TPU v7x, 32 devices: a whole 2x2x4 slice. The times are simulated.
32 devices in a mesh: shard: 2 (over y), ctx: 4 (over x, core), tensor: 4 (over z).
Axes of the slice: x: 2, y: 2, z: 4, core: 2. Of those that a mesh axis runs over, the one named last changes fastest.
Arguments:
- inputs: bfloat16 [2, 1024, 2048], P('shard', 'ctx'), may hold values from -6 to 6
- cotangent: bfloat16 [2, 1024, 2048], P('shard', 'ctx'), may hold values from -6 to 6
- piece_starts: int32 [2, 3], P('shard'), may hold values from 0 to 768, as said below
- positions: int32 [2, 1024], P('shard', 'ctx'), may hold values from 0 to 303, as said below
- w_qkv: float32 [2048, 8, 768], P(('shard', 'ctx'), 'tensor'), may hold values from -0.125 to 0.125
- b_qkv: float32 [8, 768], P('tensor'), may hold values from -1.2 to 1.2
- w_dense: float32 [2048, 8, 256], P(('shard', 'ctx'), 'tensor'), may hold values from -0.5 to 0.5
- w_fc1: float32 [2048, 8192], P(('shard', 'ctx'), 'tensor'), may hold values from -0.125 to 0.125
- b_fc1: float32 [8192], P('tensor'), may hold values from -3 to 3
- w_fc2: float32 [2048, 8192], P(('shard', 'ctx'), 'tensor'), may hold values from -0.0625 to 0.0625
- out_bias: float32 [2048], replicated, may hold values from -3 to 3
- ln1_gain: float32 [2048], replicated, may hold values from 0.1 to 1.9
- ln1_bias: float32 [2048], replicated, may hold values from -2 to 2
- ln2_gain: float32 [2048], replicated, may hold values from 0.1 to 1.9
- ln2_bias: float32 [2048], replicated, may hold values from -2 to 2
Outputs:
- output: bfloat16 [2, 1024, 2048], P('shard', 'ctx')
- grad_inputs: float32 [2, 1024, 2048], P('shard', 'ctx')
- grad_w_qkv: float32 [2048, 8, 768], P(('shard', 'ctx'), 'tensor')
- grad_b_qkv: float32 [8, 768], P('tensor')
- grad_w_dense: float32 [2048, 8, 256], P(('shard', 'ctx'), 'tensor')
- grad_w_fc1: float32 [2048, 8192], P(('shard', 'ctx'), 'tensor')
- grad_b_fc1: float32 [8192], P('tensor')
- grad_w_fc2: float32 [2048, 8192], P(('shard', 'ctx'), 'tensor')
- grad_out_bias: float32 [2048], replicated
- grad_ln1_gain: float32 [2048], replicated
- grad_ln1_bias: float32 [2048], replicated
- grad_ln2_gain: float32 [2048], replicated
- grad_ln2_bias: float32 [2048], replicated
Inputs may be any that keep to these rules, and one draw needn't show every extreme that they name: `piece_starts`: for each sequence, 3 starts in increasing order; its picture pieces of 256 tokens do not intersect and lie inside the sequence. `positions`: in each sequence the position starts at 0 and rises by one at every token outside the picture pieces and at the first of every 16 tokens of a piece; the other tokens of a piece keep the position before them.
All inputs are finite; a program needn't handle non-finite values.
Results may differ from a plain program's by a relative error of at most 0.012.
Values may be sent and summed in bfloat16 or wider, within the bound.
No kernel may reach another device: no remote copies, remote signals or barrier semaphores. Data moves between devices by JAX's collectives and lax.ppermute only.
A program may use at most 256 MiB of HBM per device.

v0:
```python
import jax
import jax.numpy as jnp
from jax import lax
from jax.sharding import PartitionSpec as P

HEAD = 256
ROT = 64
PIECE = 256
PIECES = 3


EPSILON = 1e-05
ROPE_BASE = 10000.0


def layer_norm(values, norm_gain, norm_shift):
    centred = values - jnp.mean(values, axis=-1, keepdims=True)
    spread = jnp.mean(centred * centred, axis=-1, keepdims=True)
    return centred * lax.rsqrt(spread + EPSILON) * norm_gain + norm_shift


def rotary_tables(places):
    half_rot = ROT // 2
    frequency = ROPE_BASE ** (-(jnp.arange(half_rot, dtype=jnp.float32) * 2.0) / ROT)
    angles = places.astype(jnp.float32)[..., None] * frequency
    angles = jnp.concatenate([angles, angles], axis=-1)
    return (jnp.cos(angles)[..., None, :], jnp.sin(angles)[..., None, :])


def rotate(head_values, cosine, sine_part):
    half_rot = ROT // 2
    rotated_part = head_values[..., :ROT]
    turned = jnp.concatenate([-rotated_part[..., half_rot:], rotated_part[..., :half_rot]], axis=-1)
    return jnp.concatenate(
        [rotated_part * cosine + turned * sine_part, head_values[..., ROT:]], axis=-1
    )


def piece_map(token_index, starts):
    inside = (token_index[None, :, None] >= starts[:, None, :]) & (
        token_index[None, :, None] < starts[:, None, :] + PIECE
    )
    labels = jnp.arange(1, PIECES + 1, dtype=jnp.int32)
    return jnp.sum(jnp.where(inside, labels, 0), axis=2)


def exact_gelu(pre_act):
    return jax.nn.gelu(pre_act, approximate=False)


def cross_rows(left_rows, right_rows):
    return lax.dot_general(
        left_rows, right_rows, (((1,), (1,)), ((), ())), preferred_element_type=jnp.float32
    )


def outer_rows(left_rows, right_rows):
    return lax.dot_general(
        left_rows, right_rows, (((0,), (0,)), ((), ())), preferred_element_type=jnp.float32
    )


def local(
    inputs,
    cotangent,
    piece_starts,
    positions,
    w_qkv,
    b_qkv,
    w_dense,
    w_fc1,
    b_fc1,
    w_fc2,
    out_bias,
    ln1_gain,
    ln1_bias,
    ln2_gain,
    ln2_bias,
):
    groups, seq_span, model_width = inputs.shape
    row_count = groups * seq_span
    local_heads = w_qkv.shape[1]
    shard_rows = w_qkv.shape[0]
    seq_length = seq_span * lax.axis_size("ctx")
    score_scale = HEAD ** (-0.5)
    attn_cols = local_heads * HEAD
    joint_cols = local_heads * 3 * HEAD
    residual = inputs.astype(jnp.float32).reshape(row_count, model_width)
    normed_one = layer_norm(residual, ln1_gain, ln1_bias).astype(jnp.bfloat16)
    normed_two = layer_norm(residual, ln2_gain, ln2_bias).astype(jnp.bfloat16)
    qkv_low = w_qkv.astype(jnp.bfloat16)
    dense_low = w_dense.astype(jnp.bfloat16)
    fc1_low = w_fc1.astype(jnp.bfloat16)
    fc2_low = w_fc2.astype(jnp.bfloat16)
    front_qkv, front_fc1 = (
        lax.all_gather(qkv_low, ("shard", "ctx"), axis=0, tiled=True),
        lax.all_gather(fc1_low, ("shard", "ctx"), axis=0, tiled=True),
    )
    joined = jnp.dot(
        normed_one, front_qkv.reshape(model_width, joint_cols), preferred_element_type=jnp.float32
    )
    inner_sum = jnp.dot(normed_two, front_fc1, preferred_element_type=jnp.float32)
    joined = joined.reshape(groups, seq_span, local_heads, 3 * HEAD) + b_qkv
    cosine, sine_part = rotary_tables(positions)
    queries = rotate(joined[..., :HEAD], cosine, sine_part).astype(jnp.bfloat16)
    key_rows = rotate(joined[..., HEAD : 2 * HEAD], cosine, sine_part).astype(jnp.bfloat16)
    value_rows = joined[..., 2 * HEAD :].astype(jnp.bfloat16)
    all_keys, all_values = (
        lax.all_gather(key_rows, "ctx", axis=1, tiled=True),
        lax.all_gather(value_rows, "ctx", axis=1, tiled=True),
    )
    key_index = jnp.arange(seq_length, dtype=jnp.int32)
    query_index = lax.axis_index("ctx") * seq_span + jnp.arange(seq_span, dtype=jnp.int32)
    key_piece = piece_map(key_index, piece_starts)
    query_piece = piece_map(query_index, piece_starts)
    allowed = (key_index[None, None, :] <= query_index[None, :, None]) | (
        key_piece[:, None, :] == query_piece[:, :, None]
    ) & (query_piece[:, :, None] > 0)

    def score_block(query_low):
        raw_scores = (
            jnp.einsum("gqhd,gkhd->ghqk", query_low, all_keys, preferred_element_type=jnp.float32)
            * score_scale
        )
        return jnp.where(allowed[:, None], raw_scores, -1e30)

    scores = score_block(queries)
    row_max = jnp.max(scores, axis=-1, keepdims=True)
    exponent = jnp.exp(scores - row_max)
    row_total = jnp.sum(exponent, axis=-1, keepdims=True)
    weights = exponent / row_total
    log_total = row_max + jnp.log(row_total)
    attended = jnp.einsum(
        "ghqk,gkhd->gqhd",
        weights.astype(jnp.bfloat16),
        all_values,
        preferred_element_type=jnp.float32,
    )
    context = attended.reshape(row_count, attn_cols).astype(jnp.bfloat16)
    pre_gelu = inner_sum + b_fc1
    hidden = exact_gelu(pre_gelu).astype(jnp.bfloat16)
    piece_pair = (
        lax.all_gather(dense_low, ("shard", "ctx"), axis=0, tiled=True),
        lax.all_gather(fc2_low, ("shard", "ctx"), axis=0, tiled=True),
    )
    row_span = piece_pair[0].shape[0]
    block_out = cross_rows(context, piece_pair[0].reshape(row_span, attn_cols)) + cross_rows(
        hidden, piece_pair[1]
    )
    summed_out = lax.psum(block_out, "tensor")
    output = (
        (residual + summed_out + out_bias)
        .astype(jnp.bfloat16)
        .reshape(groups, seq_span, model_width)
    )
    grad_low = cotangent.reshape(row_count, model_width)
    grad_flat = grad_low.astype(jnp.float32)
    back_dense, back_fc2 = (
        lax.all_gather(dense_low, ("shard", "ctx"), axis=0, tiled=True),
        lax.all_gather(fc2_low, ("shard", "ctx"), axis=0, tiled=True),
    )
    grad_context = jnp.dot(
        grad_low, back_dense.reshape(model_width, attn_cols), preferred_element_type=jnp.float32
    )
    grad_hidden = jnp.dot(grad_low, back_fc2, preferred_element_type=jnp.float32)
    outer_sum = lax.psum_scatter(
        jnp.concatenate([outer_rows(grad_low, context), outer_rows(grad_low, hidden)], axis=1),
        ("shard", "ctx"),
        scatter_dimension=0,
        tiled=True,
    )
    grad_w_dense = outer_sum[:, :attn_cols].reshape(shard_rows, local_heads, HEAD)
    grad_w_fc2 = outer_sum[:, attn_cols:]
    gelu_value, gelu_back = jax.vjp(exact_gelu, pre_gelu)
    grad_inner = gelu_back(grad_hidden)[0].astype(jnp.bfloat16)
    grad_mixed = grad_context.astype(jnp.bfloat16).reshape(groups, seq_span, local_heads, HEAD)
    probs_again = jnp.exp(score_block(queries) - log_total)
    grad_probs = jnp.einsum(
        "gqhd,gkhd->ghqk", grad_mixed, all_values, preferred_element_type=jnp.float32
    )
    centre = jnp.sum(probs_again * grad_probs, axis=-1, keepdims=True)
    grad_scores = (probs_again * (grad_probs - centre)).astype(jnp.bfloat16)
    grad_queries = (
        jnp.einsum("ghqk,gkhd->gqhd", grad_scores, all_keys, preferred_element_type=jnp.float32)
        * score_scale
    )
    key_terms = (
        jnp.einsum("ghqk,gqhd->gkhd", grad_scores, queries, preferred_element_type=jnp.float32)
        * score_scale
    )
    value_terms = jnp.einsum(
        "ghqk,gqhd->gkhd",
        probs_again.astype(jnp.bfloat16),
        grad_mixed,
        preferred_element_type=jnp.float32,
    )
    grad_keys, grad_values = (
        lax.psum_scatter(key_terms, "ctx", scatter_dimension=1, tiled=True),
        lax.psum_scatter(value_terms, "ctx", scatter_dimension=1, tiled=True),
    )
    back_query = rotate(grad_queries, cosine, -sine_part)
    back_key = rotate(grad_keys, cosine, -sine_part)
    grad_joined = (
        jnp.concatenate([back_query, back_key, grad_values], axis=-1)
        .reshape(row_count, joint_cols)
        .astype(jnp.bfloat16)
    )
    piece_pair = (
        lax.all_gather(qkv_low, ("shard", "ctx"), axis=0, tiled=True),
        lax.all_gather(fc1_low, ("shard", "ctx"), axis=0, tiled=True),
    )
    row_span = piece_pair[0].shape[0]
    block_one = cross_rows(grad_joined, piece_pair[0].reshape(row_span, joint_cols))
    block_two = cross_rows(grad_inner, piece_pair[1])
    grad_norm_one = block_one
    grad_norm_two = block_two
    inner_grads = lax.psum_scatter(
        jnp.concatenate(
            [outer_rows(normed_one, grad_joined), outer_rows(normed_two, grad_inner)], axis=1
        ),
        ("shard", "ctx"),
        scatter_dimension=0,
        tiled=True,
    )
    grad_w_qkv = inner_grads[:, :joint_cols].reshape(shard_rows, local_heads, 3 * HEAD)
    grad_w_fc1 = inner_grads[:, joint_cols:]
    grad_norm_one, grad_norm_two = lax.psum((grad_norm_one, grad_norm_two), "tensor")
    norm_value_one, norm_back_one = jax.vjp(layer_norm, residual, ln1_gain, ln1_bias)
    norm_value_two, norm_back_two = jax.vjp(layer_norm, residual, ln2_gain, ln2_bias)
    grad_res_one, grad_gain_one, grad_shift_one = norm_back_one(grad_norm_one)
    grad_res_two, grad_gain_two, grad_shift_two = norm_back_two(grad_norm_two)
    grad_inputs = (grad_flat + grad_res_one + grad_res_two).reshape(groups, seq_span, model_width)
    bias_qkv_term = jnp.sum(grad_joined.astype(jnp.float32), axis=0).reshape(local_heads, 3 * HEAD)
    bias_fc1_term = jnp.sum(grad_inner.astype(jnp.float32), axis=0)
    small_sums = lax.psum(
        (
            bias_qkv_term,
            bias_fc1_term,
            jnp.sum(grad_flat, axis=0),
            grad_gain_one,
            grad_shift_one,
            grad_gain_two,
            grad_shift_two,
        ),
        ("shard", "ctx"),
    )
    return (
        output,
        grad_inputs,
        grad_w_qkv,
        small_sums[0],
        grad_w_dense,
        grad_w_fc1,
        small_sums[1],
        grad_w_fc2,
        small_sums[2],
        small_sums[3],
        small_sums[4],
        small_sums[5],
        small_sums[6],
    )


def solution(mesh):
    in_specs = (
        P("shard", "ctx", None),
        P("shard", "ctx", None),
        P("shard", None),
        P("shard", "ctx"),
        P(("shard", "ctx"), "tensor", None),
        P("tensor", None),
        P(("shard", "ctx"), "tensor", None),
        P(("shard", "ctx"), "tensor"),
        P("tensor"),
        P(("shard", "ctx"), "tensor"),
        P(),
        P(),
        P(),
        P(),
        P(),
    )
    out_specs = (
        P("shard", "ctx", None),
        P("shard", "ctx", None),
        P(("shard", "ctx"), "tensor", None),
        P("tensor", None),
        P(("shard", "ctx"), "tensor", None),
        P(("shard", "ctx"), "tensor"),
        P("tensor"),
        P(("shard", "ctx"), "tensor"),
        P(),
        P(),
        P(),
        P(),
        P(),
    )
    return jax.shard_map(local, mesh=mesh, in_specs=in_specs, out_specs=out_specs, check_vma=False)
```

profile of v0, /device:TPU:0, one launch (start us, length us, event | category | flops | bytes accessed | tf_op | source)
XLA Modules:
  0.0 873.9 jit_solution(4241122452107551407)
XLA Ops:
  7.3 2.9 convert_element_type.123
  10.3 0.9 convert_element_type.130
  11.4 1.2 fusion.70
  13.3 45.5 %all-gather.7.cloned.1.call-done = bf16[2048,2,768]{2,1,0:T(2,128)(2,1)} async-done(((bf16[256,2,768]{2,1,0:T(2,128)(2,1)}), bf16[2048,2,768]{2,1,0:T(2,128)(2,1)}) %all-gather.7.cloned.1.call-update) | async-done | bytes 6291472 | tf_op jit(solution)/shard_map/all_gather | solution.py:96
  58.8 6.8 copy.109
  65.5 8.8 %copy.74 = bf16[2048,1536]{0,1:T(8,128)(2,1)} copy(bf16[2048,1536]{1,0:T(8,128)(2,1)} %bitcast.158) | data formatting | bytes 12582912 | tf_op jit(solution)/shard_map/reshape | solution.py:100
  74.3 4.6 fusion.81
  79.0 0.9 slice_bitcast_fusion
  82.0 1.7 slice.103
  83.7 1.1 convert_element_type.132
  84.9 2.7 convert_element_type.134
  88.0 1.1 fusion.53
  89.1 2.1 copy.110
  91.3 1.3 copy-done.4
  93.5 14.6 %all-gather.11.cloned.1.call-done = bf16[1,1024,2,256]{3,1,2,0:T(8,128)(2,1)} async-done(((bf16[1,256,2,256]{3,1,2,0:T(8,128)(2,1)}), bf16[1,1024,2,256]{3,1,2,0:T(8,128)(2,1)}) %all-gather.11.cloned.1.call-update) | async-done | bytes 1048592 | tf_op jit(solution)/shard_map/all_gather | solution.py:109
  108.1 2.0 fusion.82
  111.2 15.6 %all-gather.9.cloned.1.call-done = bf16[1,1024,2,256]{3,1,2,0:T(8,128)(2,1)} async-done(((bf16[1,256,2,256]{3,1,2,0:T(8,128)(2,1)}), bf16[1,1024,2,256]{3,1,2,0:T(8,128)(2,1)}) %all-gather.9.cloned.1.call-update) | async-done | bytes 1048592 | tf_op jit(solution)/shard_map/all_gather | solution.py:110
  126.8 1.7 multiply_reduce_fusion
  129.1 1.0 copy-done.3
  130.1 1.9 multiply_bitcast_fusion
  132.5 2.1 fusion.34
  136.2 1.8 copy.90
  138.0 1.9 convolution_bitcast_fusion.2
  139.9 1.9 slice_negate_fusion.1
  141.9 2.0 convolution_convert_fusion
  143.9 39.7 %all-gather.15.cloned.1.call-done = bf16[2048,2048]{1,0:T(8,128)(2,1)} async-done(((bf16[256,2048]{1,0:T(8,128)(2,1)}), bf16[2048,2048]{1,0:T(8,128)(2,1)}) %all-gather.15.cloned.1.call-update) | async-done | bytes 8388624 | tf_op jit(solution)/shard_map/all_gather | solution.py:97
  183.6 7.1 convolution_add_fusion.1
  190.7 49.6 %all-gather.17.cloned.1.call-done = bf16[2048,2048]{1,0:T(8,128)(2,1)} async-done(((bf16[256,2048]{1,0:T(8,128)(2,1)}), bf16[2048,2048]{1,0:T(8,128)(2,1)}) %all-gather.17.cloned.1.call-update) | async-done | bytes 8388624 | tf_op jit(solution)/shard_map/all_gather | solution.py:144
  240.3 10.6 %fusion.78 = f32[256,2048]{1,0:T(8,128)S(1)} fusion(bf16[2048,2048]{1,0:T(8,128)(2,1)} %all-gather.17.cloned.1.call-done, f32[256,2048]{1,0:T(8,128)} %convolution_add_fusion.1), kind=kOutput, calls=%fused_computation.149 | convolution fusion | flops 2181562368 | bytes 12582912 | tf_op jit(solution)/shard_map/dot_general | solution.py:52
  250.9 2.1 convolution_add_fusion
  253.0 8.2 convert_reduce_fusion.2
  261.2 1.0 copy-done.14
  262.2 3.7 fusion.84
  265.9 8.4 reduce-scatter.5.cloned.1.call-done
  274.3 1.3 slice.153
  276.4 1.2 slice_negate_fusion
  277.6 1.8 fusion.55
  279.4 1.0 copy.91
  280.4 1.0 copy.89
  281.4 1.0 constant_dynamic-update-slice_fusion.2
  282.4 0.9 constant_dynamic-update-slice_fusion
  283.4 25.1 %reduce-scatter.7.cloned.1.call-done = f32[1,256,2,256]{1,3,2,0:T(8,128)} async-done(((f32[1,1024,2,256]{1,3,2,0:T(8,128)}), f32[1,256,2,256]{1,3,2,0:T(8,128)}) %reduce-scatter.7.cloned.1.call-update) | async-done | bytes 524304 | tf_op jit(solution)/shard_map/reduce_scatter | solution.py:199
  308.5 1.1 convert_dynamic-update-slice_fusion
  309.5 6.0 fusion.83
  315.8 0.9 copy-done.10
  318.4 6.6 convolution_bitcast_fusion
  325.0 11.0 %pad_maximum_fusion.1 = f32[2048,2560]{0,1:T(8,128)} fusion(f32[2048,2048]{0,1:T(8,128)S(1)} %convolution_bitcast_fusion, f32[2048,512]{0,1:T(8,128)S(1)} %convolution_bitcast_fusion.1), kind=kLoop, calls=%fused_computation.1 | loop fusion | flops 5242880 | bytes 41943040 | tf_op jit(solution)/shard_map/concatenate | solution.py:167
  336.7 3.8 fusion.73
  340.5 2.0 fusion.50
  342.4 12.3 %pad_maximum_fusion = f32[2048,3584]{0,1:T(8,128)} fusion(f32[2048,2048]{0,1:T(8,128)S(1)} %fusion.73, f32[2048,1536]{0,1:T(8,128)S(1)} %fusion.50), kind=kLoop, calls=%fused_computation | loop fusion | flops 7340032 | bytes 58720256 | tf_op jit(solution)/shard_map/concatenate | solution.py:218
  355.0 184.3 %all-reduce.4.cloned.1.call-done = (f32[256,2048]{1,0:T(8,128)}, f32[256,2048]{1,0:T(8,128)}, f32[256,2048]{1,0:T(8,128)}) async-done(((f32[256,2048]{1,0:T(8,128)}, f32[256,2048]{1,0:T(8,128)}, f32[256,2048]{1,0:T(8,128)}), (f32[256,2048]{1,0:T(8,128)}, f32[256,2048]{1,0:T(8,128)}, f32[256,2048]{1,0:T(8,128)})) %all-reduce.4.cloned.1.call-update) | async-done | bytes 6291472 | tf_op jit(solution)/shard_map/psum | solution.py:150
  539.3 3.2 fusion.80
  542.8 1.7 fusion.16
  544.6 3.3 convert_reduce_fusion.1
  547.8 25.1 %all-reduce = (f32[2,768]{1,0:T(2,128)}, f32[2048]{0:T(1024)}, f32[2048]{0:T(1024)}, f32[2048]{0:T(1024)}, f32[2048]{0:T(1024)}, /*index=5*/f32[2048]{0:T(1024)}, f32[2048]{0:T(1024)}) all-reduce(f32[2,768]{1,0:T(2,128)S(1)} %convert_reduce_fusion.3, ...), channel_id=1, replica_groups=mesh['shard'=2,'ctx'=4,'tensor'=4] {'shard','ctx'}, use_global_device_ids=true, to_apply=%region_18.19 | all-reduce | flops 13824 | bytes 110592 | tf_op jit(solution)/shard_map/psum | solution.py:235
  572.9 104.7 %reduce-scatter.11.cloned.1.call-done = f32[256,2560]{0,1:T(8,128)} async-done(((f32[2048,2560]{0,1:T(8,128)}), f32[256,2560]{0,1:T(8,128)}) %reduce-scatter.11.cloned.1.call-update) | async-done | bytes 2621456 | tf_op jit(solution)/shard_map/reduce_scatter | solution.py:166
  677.7 1.6 slice-done
  679.3 1.8 copy.96
  681.1 1.0 copy.94
  682.1 178.0 %reduce-scatter.9.cloned.1.call-done = f32[256,3584]{0,1:T(8,128)} async-done(((f32[2048,3584]{0,1:T(8,128)}), f32[256,3584]{0,1:T(8,128)}) %reduce-scatter.9.cloned.1.call-update) | async-done | bytes 3670032 | tf_op jit(solution)/shard_map/reduce_scatter | solution.py:217
  860.1 1.6 slice-done.2
  861.7 1.8 copy.95
  863.5 1.4 slice-done.3
  864.9 2.1 copy.93
  (145 shorter events, 12.2 us)
Async XLA Ops:
  7.2 3.1 copy-start.20
  7.2 4.0 copy-start.38
  7.2 5.4 copy-start
  7.2 51.5 %all-gather.7.cloned.1.call-start = ((), (), s32[]{:S(2)}) async-start(), calls=%async_computation.4 | async-start | bytes 7077888 | tf_op jit(solution)/shard_map/all_gather | solution.py:96
  10.2 78.9 %all-gather.13.cloned.1.call-start = ((), (), s32[]{:S(2)}) async-start(), calls=%async_computation.7 | async-start | bytes 2359296 | tf_op jit(solution)/shard_map/all_gather | solution.py:143
  11.2 96.9 %all-gather.11.cloned.1.call-start = ((), (), s32[]{:S(2)}) async-start(), calls=%async_computation.6 | async-start | bytes 1310720 | tf_op jit(solution)/shard_map/all_gather | solution.py:109
  12.8 61.5 %copy-start.24 = (f32[256]{0:T(256)}, f32[256]{0:T(256)S(1)}, u32[]{:S(2)}) copy-start(f32[256]{0:T(256)S(1)} %broadcast_multiply_fusion.1) | copy-start | bytes 3076
  13.3 52.3 %copy-start.28 = (f32[256]{0:T(256)}, f32[256]{0:T(256)S(1)}, u32[]{:S(2)}) copy-start(f32[256]{0:T(256)S(1)} %fusion.17) | copy-start | bytes 3076
  13.3 61.0 %copy-start.26 = (f32[256]{0:T(256)}, f32[256]{0:T(256)S(1)}, u32[]{:S(2)}) copy-start(f32[256]{0:T(256)S(1)} %fusion.67) | copy-start | bytes 3076
  65.5 8.8 %copy-start.22 = (f32[2048]{0:T(1024)S(1)}, f32[2048]{0:T(1024)}, u32[]{:S(2)}) copy-start(f32[2048]{0:T(1024)} %param.26) | copy-start | bytes 24580
  65.5 8.8 %copy-start.30 = (f32[2048]{0:T(1024)S(1)}, f32[2048]{0:T(1024)}, u32[]{:S(2)}) copy-start(f32[2048]{0:T(1024)} %param.27) | copy-start | bytes 24580
  65.5 8.8 %copy-start.40 = (f32[2,768]{1,0:T(2,128)S(1)}, f32[2,768]{1,0:T(2,128)}, u32[]{:S(2)}) copy-start(f32[2,768]{1,0:T(2,128)} %param.20) | copy-start | bytes 18436
  79.0 2.1 copy-start.18
  79.0 1.2 copy-start.21
  80.2 3.6 copy-start.11
  81.9 44.9 %all-gather.9.cloned.1.call-start = ((), (), s32[]{:S(2)}) async-start(), calls=%async_computation.5 | async-start | bytes 1310720 | tf_op jit(solution)/shard_map/all_gather | solution.py:110
  83.7 99.9 %all-gather.15.cloned.1.call-start = ((), (), s32[]{:S(2)}) async-start(), calls=%async_computation.8 | async-start | bytes 9437184 | tf_op jit(solution)/shard_map/all_gather | solution.py:97
  84.9 2.9 copy-start.37
  84.9 155.4 %all-gather.17.cloned.1.call-start = ((), (), s32[]{:S(2)}) async-start(), calls=%async_computation.9 | async-start | bytes 9437184 | tf_op jit(solution)/shard_map/all_gather | solution.py:144
  87.7 186.6 %reduce-scatter.5.cloned.1.call-start = ((), (), s32[]{:S(2)}) async-start(), calls=%async_computation.10 | async-start | bytes 2621440 | tf_op jit(solution)/shard_map/reduce_scatter | solution.py:198
  89.1 3.5 copy-start.8
  91.3 1.3 copy-start.4
  110.0 0.6 copy-start.34
  110.6 0.6 copy-start.35
  128.5 1.5 copy-start.15
  128.5 1.5 copy-start.19
  129.1 1.0 copy-start.3
  132.0 176.4 %reduce-scatter.7.cloned.1.call-start = ((), (), s32[]{:S(2)}) async-start(), calls=%async_computation.11 | async-start | bytes 2621440 | tf_op jit(solution)/shard_map/reduce_scatter | solution.py:199
  134.6 0.8 copy-start.6
  141.9 41.7 %copy-start.23 = (f32[2048]{0:T(1024)S(1)}, f32[2048]{0:T(1024)}, u32[]{:S(2)}) copy-start(f32[2048]{0:T(1024)} %param.28) | copy-start | bytes 24580
  141.9 397.4 %all-reduce.4.cloned.1.call-start = ((), (), s32[]{:S(2)}) async-start(), calls=%async_computation.14 | async-start | bytes 12582912 | tf_op jit(solution)/shard_map/psum | solution.py:150
  190.7 60.2 %copy-start.5 = (bf16[256,8,2,256]{3,1,2,0:T(8,128)(2,1)S(1)}, bf16[256,8,2,256]{3,1,2,0:T(8,128)(2,1)}, u32[]{:S(2)}) copy-start(bf16[256,8,2,256]{3,1,2,0:T(8,128)(2,1)} %copy-done.4) | copy-start | bytes 6291460
  240.3 12.7 %copy-start.39 = (bf16[2048,2048]{1,0:T(8,128)(2,1)S(1)}, bf16[2048,2048]{1,0:T(8,128)(2,1)}, u32[]{:S(2)}) copy-start(bf16[2048,2048]{1,0:T(8,128)(2,1)} %all-gather.17.cloned.1.call-done) | copy-start | bytes 25165828
  240.3 12.7 %copy-start.41 = (f32[256,2048]{1,0:T(8,128)S(1)}, f32[256,2048]{1,0:T(8,128)}, u32[]{:S(2)}) copy-start(f32[256,2048]{1,0:T(8,128)} %convolution_add_fusion.1) | copy-start | bytes 6291460
  250.9 2.1 copy-start.9
  250.9 11.3 %slice-start.4 = ((s8[8388608]{0:T(1024)(128)(4,1)}), s8[4194304]{0:T(1024)(128)(4,1)S(1)}, s32[]{:S(2)}) async-start(s8[8388608]{0:T(1024)(128)(4,1)} %bitcast.176), calls=%async_computation.19 | async-start | bytes 8388608
  253.0 9.2 %slice-start.5 = ((s8[8388608]{0:T(1024)(128)(4,1)}), s8[4194304]{0:T(1024)(128)(4,1)S(1)}, s32[]{:S(2)}) async-start(s8[8388608]{0:T(1024)(128)(4,1)} %bitcast.176), calls=%async_computation.20 | async-start | bytes 8388608
  261.2 1.0 copy-start.14
  265.9 11.7 %copy-start.7 = (f32[1,256,2,256]{3,1,2,0:T(8,128)S(1)}, f32[1,256,2,256]{3,1,2,0:T(8,128)}, u32[]{:S(2)}) copy-start(f32[1,256,2,256]{3,1,2,0:T(8,128)} %copy-done.6) | copy-start | bytes 1572868
  265.9 11.7 %copy-start.16 = (f32[1,256,2,32]{3,1,2,0:T(8,128)S(1)}, f32[1,256,2,32]{3,1,2,0:T(8,128)}, u32[]{:S(2)}) copy-start(f32[1,256,2,32]{3,1,2,0:T(8,128)} %get-tuple-element.89) | copy-start | bytes 196612
  265.9 11.7 %copy-start.17 = (f32[1,256,2,32]{3,1,2,0:T(8,128)S(1)}, f32[1,256,2,32]{3,1,2,0:T(8,128)}, u32[]{:S(2)}) copy-start(f32[1,256,2,32]{3,1,2,0:T(8,128)} %get-tuple-element.90) | copy-start | bytes 196612
  274.3 3.3 copy-start.13
  315.5 1.2 copy-start.10
  315.6 362.1 %reduce-scatter.11.cloned.1.call-start = ((), (), s32[]{:S(2)}) async-start(), calls=%async_computation.13 | async-start | bytes 23592960 | tf_op jit(solution)/shard_map/reduce_scatter | solution.py:166
  316.8 1.6 copy-start.42
  335.9 0.7 copy-start.25
  335.9 0.7 copy-start.27
  335.9 0.7 copy-start.32
  336.0 4.5 copy-start.31
  336.0 524.1 %reduce-scatter.9.cloned.1.call-start = ((), (), s32[]{:S(2)}) async-start(), calls=%async_computation.12 | async-start | bytes 33030144 | tf_op jit(solution)/shard_map/reduce_scatter | solution.py:217
  539.3 3.2 copy-start.29
  539.3 3.3 copy-start.1
  539.3 3.5 copy-start.2
  542.8 1.8 copy-start.12
  542.8 1.8 copy-start.36
  544.5 3.3 copy-start.33
  677.7 1.6 slice-start
  679.3 1.8 slice-start.1
  860.1 1.6 slice-start.2
  863.5 1.4 slice-start.3
Sparse Core Ops, SparseCore 0:
  10.5 48.2 all-gather.6
  61.2 27.8 all-gather.12
  91.3 16.7 all-gather.10
  110.1 16.7 all-gather.8
  129.1 54.3 all-gather.14
  185.9 54.3 all-gather.16
  242.8 31.4 reduce-scatter.4
  277.0 31.4 reduce-scatter.6
  315.7 223.5 all-reduce.3
  542.7 134.8 reduce-scatter.10
  681.3 178.7 reduce-scatter.8
where the time goes:
time: 883 us; the launch traced here: 874 us
  waiting for transfers between devices  666 us (75%)
  matrix products  67.5 us (8%)
  other arithmetic  51.4 us (6%)
  local copies, waits for them, and re-layouts  47.8 us (5%)
  blocking collectives  25.1 us (3%)
  between operations  14.9 us (2%)
    psum x1, waiting for transfers between devices, local(): summed_out = lax.psum(block_out, 'tensor')  184 us
    reduce_scatter x1, waiting for transfers between devices, local(): lax.psum_scatter(jnp.concatenate([outer_rows(normed_one, grad_joined), ou...  178 us
    reduce_scatter x1, waiting for transfers between devices, local(): lax.psum_scatter(jnp.concatenate([outer_rows(grad_low, context), outer_ro...  105 us
    all_gather x1, waiting for transfers between devices, local(): lax.all_gather(fc2_low, ('shard', 'ctx'), axis=0, tiled=True)  49.6 us
    all_gather x1, waiting for transfers between devices, local(): lax.all_gather(qkv_low, ('shard', 'ctx'), axis=0, tiled=True)  45.5 us
    all_gather x1, waiting for transfers between devices, local(): lax.all_gather(fc1_low, ('shard', 'ctx'), axis=0, tiled=True)  39.7 us
    psum x1, blocking collectives, local(): lax.psum((bias_qkv_term, bias_fc1_term, jnp.sum(grad_flat, axis=0), grad_...  25.1 us
    reduce_scatter x1, waiting for transfers between devices, local(): lax.psum_scatter(value_terms, 'ctx', scatter_dimension=1, tiled=True)  25.1 us
  transfers between devices with their start and end apart: 11, of which 11 were waited for; matrix products, arithmetic and copies ran while one was open for 16% of the time, Pallas kernels for 0%

commit v1 on v0

v1 whole, which is shorter than its diff:
```python
import functools

import jax
import jax.numpy as jnp
import numpy as np
from jax import lax
from jax.experimental import pallas as pl
from jax.experimental.pallas import tpu as pltpu
from jax.sharding import PartitionSpec as P

HEAD = 256
HALF = HEAD // 2
ROT = 64
PIECE = 256
GRID = 16
PIECES = 3

EPSILON = 1e-05
ROPE_BASE = 10000.0
ORDER = (0, 2, 1, 3)
BF16 = jnp.bfloat16
F32 = jnp.float32
VMEM = pl.BlockSpec(memory_space=pltpu.VMEM)
SMEM = pl.BlockSpec(memory_space=pltpu.SMEM)


def dot(left, right, dims):
    return lax.dot_general(left, right, ((dims[:1], dims[1:]), ((), ())), preferred_element_type=F32)


def shape(*dims, kind=BF16):
    return jax.ShapeDtypeStruct(dims, kind)


def call(kernel, outs, args, flops=0, grid=None, in_specs=None, out_specs=None, scratch=(), limit=40, prefetch=0):
    if grid is None:
        extra = dict(in_specs=[SMEM] * (1 + prefetch) + [VMEM] * (len(args) - 1 - prefetch), out_specs=[VMEM] * len(outs), scratch_shapes=scratch)
    else:
        extra = dict(grid_spec=pltpu.PrefetchScalarGridSpec(num_scalar_prefetch=1 + prefetch, grid=grid, in_specs=in_specs, out_specs=out_specs, scratch_shapes=scratch))
    size = sum(a.size * a.dtype.itemsize for a in args) + sum(int(np.prod(o.shape)) * o.dtype.itemsize for o in outs)
    return pl.pallas_call(
        kernel, out_shape=outs, compiler_params=pltpu.CompilerParams(vmem_limit_bytes=limit * 2**20),
        cost_estimate=pl.CostEstimate(flops=int(flops), bytes_accessed=int(size), transcendentals=0), **extra,
    )(*args)


def whole(array):
    return pl.BlockSpec(array.shape, lambda *_: (0,) * len(array.shape))


def swap(value, mask):
    return lax.ppermute(value, "ctx", [(i, i ^ mask) for i in range(4)])


def level_swap(value, mask):
    return lax.ppermute(value, "tensor", [(i, i ^ mask) for i in range(4)])


def shift(value, step):
    size = lax.axis_size("shard")
    return lax.ppermute(value, "shard", [(i, (i + step) % size) for i in range(size)])


def part(ref, start, size):
    return ref[:, pl.ds(pl.multiple_of(start, 128), size)]


def prepare_joint(place, qkv, dense, *outs):
    for mask, out in enumerate(outs):
        head, half = place[2] ^ (mask >> 1), place[1] ^ (mask & 1)
        out[:, :HEAD] = part(qkv, head * 3 * HEAD + half * HEAD, HEAD).astype(BF16)
        out[:, HEAD:HEAD + HALF] = part(qkv, head * 3 * HEAD + 2 * HEAD + half * HALF, HALF).astype(BF16)
        out[:, HEAD + HALF:] = part(dense, head * HEAD + half * HALF, HALF).astype(BF16)


def prepare_inner(place, one, two, own, core, one_x, one_d, two_x, two_d):
    rows, width = one_x.shape
    for mask, first, second in ((0, own.at[:rows], own.at[rows:]), (1, core.at[:rows], core.at[rows:]), (2, one_x, two_x), (3, one_d, two_d)):
        first[...] = part(one, (place[0] ^ mask) * width, width).astype(BF16)
        second[...] = part(two, (place[0] ^ mask) * width, width).astype(BF16)


def assemble(place, pieces, out, rows, shards):
    for ref, first, mask, step in pieces:
        to = lax.rem(place[3] + step, shards) * 4 * rows + (place[0] ^ mask) * rows
        out[pl.ds(pl.multiple_of(to, 16), rows), :] = ref[first:first + rows, :]


def token_block(place, step, parts, use):
    own, near, far, sib, near_sib, far_sib = parts
    same = place[4] & 1
    for base, one, first, second in ((0, own, near, far), (4, sib, near_sib, far_sib)):
        for k in (0, 1):
            pl.when(step == base + k)(lambda one=one, k=k: use(one[k * 128:(k + 1) * 128, :]))
        pl.when(step == base + 2 + same)(lambda first=first: use(first[...]))
        pl.when(step == base + 3 - same)(lambda second=second: use(second[...]))


def norm_kernel(place, own, near, far, sib, near_sib, far_sib, gain_one, shift_one, gain_two, shift_two, one, two, plain):
    def use(block):
        values = block.astype(F32)
        centred = values - jnp.mean(values, axis=1, keepdims=True)
        normal = centred * lax.rsqrt(jnp.mean(centred * centred, axis=1, keepdims=True) + EPSILON)
        one[...] = (normal * gain_one[...] + shift_one[...]).astype(BF16)
        two[...] = (normal * gain_two[...] + shift_two[...]).astype(BF16)
        plain[...] = normal.astype(BF16)

    token_block(place, pl.program_id(0), (own, near, far, sib, near_sib, far_sib), use)


def global_index(place, local, block):
    index = local
    for p in range(4):
        index = jnp.where(local // block == p, local % block + (place[0] ^ ORDER[p]) * block, index)
    return index


def turn(front, cosine, sine):
    lane = lax.broadcasted_iota(jnp.int32, front.shape, 1)
    swapped = jnp.where(lane < ROT // 2, pltpu.roll(front, HALF - ROT // 2, 1), pltpu.roll(front, ROT // 2, 1))
    return front * cosine + swapped * sine


def joint_kernel(rows, shards, pieces, place, starts, normed, bias, frequency, *refs):
    blocks, (mine, cosine, sine, weight) = refs[:-4], refs[-4:]
    step = pl.program_id(0)

    @pl.when(step == 0)
    def _():
        assemble(place, [(ref,) + p for ref, p in zip(blocks, pieces)], weight, rows, shards)

    span = normed.shape[0]
    index = lax.broadcasted_iota(jnp.int32, (span, 1), 0)
    order = jnp.where(step == 1, 2, jnp.where(step == 2, 1, step))
    index = index + (place[0] ^ order) * span
    places = index
    for j in range(PIECES):
        inside = jnp.clip(index - starts[j] + 1, 0, PIECE)
        places = places - inside + (inside + GRID - 1) // GRID
    angles = places.astype(F32) * frequency[...]
    lane = lax.broadcasted_iota(jnp.int32, (span, HALF), 1)
    cosine[...] = jnp.cos(angles)
    sine[...] = jnp.where(lane < ROT // 2, -1.0, 1.0) * jnp.sin(angles)
    joined = dot(normed[...], weight[:, :HEAD + HALF], (1, 0))
    head, half = place[2], place[1]
    joined_low = joined[:, :HEAD] + part(bias, head * 3 * HEAD + half * HEAD, HEAD)
    mine[:, :HALF] = turn(joined_low[:, :HALF], cosine[...], sine[...]).astype(BF16)
    mine[:, HALF:HEAD] = joined_low[:, HALF:].astype(BF16)
    mine[:, HEAD:] = (joined[:, HEAD:] + part(bias, head * 3 * HEAD + 2 * HEAD + half * HALF, HALF)).astype(BF16)


def context_kernel(place, own, near, far, sib, near_sib, far_sib, weight, mine, full, total):
    def use(block):
        full[...] = block
        mine[...] = dot(block, weight[:, HEAD + HALF:], (1, 0)).astype(BF16)

    token_block(place, pl.program_id(0), (own, near, far, sib, near_sib, far_sib), use)

    @pl.when(pl.program_id(0) == 0)
    def _():
        total[...] = jnp.sum(own[...].astype(F32), axis=0, keepdims=True)


def attention_kernel(place, starts, mine, got, grad_mine, grad_got, cosine, sine, context, grad, queries, keys, values, grads, acc, value_acc):
    core = place[1]
    length = mine.shape[0]
    half, block = length // 2, length // 4
    scale = HEAD ** (-0.5)
    for p in range(4):
        rows = slice(p * block, (p + 1) * block)
        first = (p * block + half) % length
        theirs = slice(first, first + block)

        @pl.when(core == 0)
        def _():
            queries[rows] = mine[rows, :HEAD]
            keys[rows] = got[theirs, :HEAD]

        @pl.when(core == 1)
        def _():
            queries[rows] = got[theirs, :HEAD]
            keys[rows] = mine[rows, :HEAD]

        values[rows, :HALF] = mine[rows, HEAD:]
        values[rows, HALF:] = got[theirs, HEAD:]
        grads[rows, :HALF] = grad_mine[rows]
        grads[rows, HALF:] = grad_got[theirs]

    def numbers(index):
        label = jnp.zeros_like(index)
        for j in range(PIECES):
            label = jnp.where((index >= starts[j]) & (index < starts[j] + PIECE), j + 1, label)
        return label

    key_index = global_index(place, lax.broadcasted_iota(jnp.int32, (1, length), 1), block)
    key_piece = numbers(key_index)
    for p in range(4):
        rows = slice(p * block, (p + 1) * block)
        query_index = lax.broadcasted_iota(jnp.int32, (block, 1), 0) + (place[0] ^ ORDER[p]) * block
        query_piece = numbers(query_index)
        allowed = (key_index <= query_index) | ((key_piece == query_piece) & (query_piece > 0))
        scores = jnp.where(allowed, dot(queries[rows], keys[...], (1, 1)) * scale, -1e30)
        weights = jnp.exp(scores - jnp.max(scores, axis=1, keepdims=True))
        weights = weights / jnp.sum(weights, axis=1, keepdims=True)
        low = weights.astype(BF16)
        context[rows] = dot(low, values[:, :HALF], (1, 0)).astype(BF16)
        term = dot(low, grads[rows, :HALF], (0, 0))
        value_acc[...] = term if p == 0 else value_acc[...] + term
        grad_weights = dot(grads[rows], values[...], (1, 1))
        centre = jnp.sum(weights * grad_weights, axis=1, keepdims=True)
        back = (weights * (grad_weights - centre)).astype(BF16)

        @pl.when(core == 0)
        def _():
            acc[rows] = dot(back, keys[...], (1, 0)) * scale

        @pl.when(core == 1)
        def _():
            term = dot(back, queries[rows], (0, 0)) * scale
            acc[...] = term if p == 0 else acc[...] + term

    grad[:, HEAD:] = value_acc[...].astype(BF16)
    grad[:, HALF:HEAD] = acc[:, HALF:].astype(BF16)
    grad[:, :HALF] = turn(acc[:, :HALF], cosine[...], -sine[...]).astype(BF16)


def hidden_kernel(rows, shards, pieces, place, normed, bias, *refs):
    blocks, (hidden, slope, weight) = refs[:-3], refs[-3:]

    @pl.when(pl.program_id(0) == 0)
    def _():
        assemble(place, [(ref,) + p for ref, p in zip(blocks, pieces)], weight, rows, shards)

    width = hidden.shape[1]
    pre = dot(normed[...], weight[...], (1, 0)) + part(bias, place[0] * width, width)
    cdf = 0.5 + 0.5 * lax.erf(pre * (0.5 ** 0.5))
    hidden[...] = (pre * cdf).astype(BF16)
    slope[...] = cdf + pre * jnp.exp(-0.5 * pre * pre) * ((0.5 / np.pi) ** 0.5)


def inner_kernel(rows, shards, pieces, place, grads, slope, *refs):
    blocks, (inner, weight) = refs[:-2], refs[-2:]

    @pl.when(pl.program_id(0) == 0)
    def _():
        assemble(place, [(ref,) + p for ref, p in zip(blocks, pieces)], weight, rows, shards)

    inner[...] = (dot(grads[...], weight[...], (1, 0)) * slope[...]).astype(BF16)


def weight_kernel(rows, shards, steps, place, *refs):
    pairs = len(refs) // 2 - 2
    lefts, rights, (near, far, own, held) = refs[:pairs], refs[pairs:2 * pairs], refs[2 * pairs:]
    turn_of, inner = pl.program_id(0), pl.program_id(1)
    size = 4 * rows // steps
    start = 0
    for left, right in zip(lefts, rights):
        width = right.shape[1]
        held[pl.ds(pl.multiple_of(inner * size, 16), size), start:start + width] = dot(left[...], right[...], (0, 0))
        start += width

    def rows_of(mask):
        return held[pl.ds(pl.multiple_of((place[0] ^ mask) * rows, 16), rows), :].astype(BF16)

    @pl.when((inner == steps - 1) & (turn_of < shards - 1))
    def _():
        near[0, :rows], near[0, rows:] = rows_of(0), rows_of(1)
        far[0, :rows], far[0, rows:] = rows_of(2), rows_of(3)

    @pl.when((inner == steps - 1) & (turn_of == shards - 1))
    def _():
        for mask in range(4):
            own[mask * rows:(mask + 1) * rows] = rows_of(mask)


def weight_grad(place, lefts, rights, rows, shards):
    width = sum(right.shape[1] for right in rights)
    length = lefts[0].shape[0]
    steps = max(1, 4 * rows // 256)
    others = max(shards - 1, 1)

    def block(turn_of, inner, place):
        step = jnp.where(turn_of == shards - 1, 0, turn_of + 1)
        return (0, lax.rem(place[3] + step, shards) * steps + inner)

    def other(turn_of, inner, place):
        return (jnp.minimum(turn_of, others - 1), 0, 0)

    near, far, own = call(
        functools.partial(weight_kernel, rows, shards, steps),
        [shape(others, 2 * rows, width), shape(others, 2 * rows, width), shape(4 * rows, width)],
        [place, *lefts, *rights], flops=2 * length * lefts[0].shape[1] * width, grid=(shards, steps),
        in_specs=[pl.BlockSpec((length, 4 * rows // steps), block)] * len(lefts) + [whole(right) for right in rights],
        out_specs=[pl.BlockSpec((1, 2 * rows, width), other)] * 2 + [pl.BlockSpec((4 * rows, width), lambda *_: (0, 0))],
        scratch=[pltpu.VMEM((4 * rows, width), F32)])
    return near, far, own


def add_two(mine, *got):
    total = mine.astype(F32)
    for value in got:
        total = total + value.astype(F32)
    return total.astype(BF16)


def reduce_weight(near, far, own, rows, shards):
    got_far = [shift(far[k - 1], k) for k in range(1, shards)]
    got_near = [shift(near[k - 1], k) for k in range(1, shards)]
    pick = lambda values, i: [value[i * rows:(i + 1) * rows] for value in values]
    cut = [own[m * rows:(m + 1) * rows] for m in range(4)]
    third = swap(add_two(cut[2], *pick(got_far, 0)), 2)
    fourth = swap(add_two(cut[3], *pick(got_far, 1)), 3)
    second = swap(add_two(cut[1], *pick(got_near, 1)), 1)
    return add_two(cut[0], *pick(got_near, 0)), second, third, fourth


def place_inner(place, *refs):
    pieces, out = refs[:-1], refs[-1]
    width = pieces[0].shape[1]
    for mask, piece in enumerate(pieces):
        out[:, pl.ds(pl.multiple_of((place[0] ^ mask) * width, 128), width)] = piece[...].astype(F32)


def place_joint(place, *refs):
    pieces, (qkv, dense) = refs[:-2], refs[-2:]
    for mask, piece in enumerate(pieces):
        head, half = place[2] ^ (mask >> 1), place[1] ^ (mask & 1)
        for out, start, size, first in ((qkv, head * 3 * HEAD + half * HEAD, HEAD, 0), (qkv, head * 3 * HEAD + 2 * HEAD + half * HALF, HALF, HEAD),
                                        (dense, head * HEAD + half * HALF, HALF, HEAD + HALF)):
            out[:, pl.ds(pl.multiple_of(start, 128), size)] = piece[:, first:first + size].astype(F32)


def output_kernel(place, context, hidden, joint, weight, keep, send):
    block = dot(context[...], joint[:, HEAD + HALF:], (1, 1)) + dot(hidden[...], weight[...], (1, 1))
    pl.when(pl.program_id(0) < 2)(lambda: keep.__setitem__(..., block.astype(BF16)))
    pl.when(pl.program_id(0) >= 2)(lambda: send.__setitem__(..., block.astype(BF16)))


def back_kernel(place, grad, inner, joint, weight, gain_one, gain_two, plain, total, keep, send, small):
    step = pl.program_id(0)
    one = dot(grad[...], joint[:, :HEAD + HALF], (1, 1))
    two = dot(inner[...], weight[...], (1, 1))
    mixed = (one * gain_one[...] + two * gain_two[...]).astype(BF16)
    pl.when(step < 2)(lambda: keep.__setitem__(..., mixed))
    pl.when(step >= 2)(lambda: send.__setitem__(..., mixed))

    @pl.when(step == 0)
    def _():
        small[...] = jnp.zeros_like(small)
        small[4:5] = total[...]

    normal = plain[...].astype(F32)
    for row, value in ((0, one * normal), (1, one), (2, two * normal), (3, two)):
        small[row:row + 1] += jnp.sum(value, axis=0, keepdims=True)
    head, half = place[2], place[1]
    joined = jnp.sum(grad[...].astype(F32), axis=0, keepdims=True)
    for first, start, size in ((0, head * 3 * HEAD + half * HEAD, HEAD), (HEAD, head * 3 * HEAD + 2 * HEAD + half * HALF, HALF)):
        small[5:6, pl.ds(pl.multiple_of(start, 128), size)] += joined[:, first:first + size]
    width = inner.shape[1]
    small[6:7, pl.ds(pl.multiple_of(place[0] * width, 128), width)] += jnp.sum(inner[...].astype(F32), axis=0, keepdims=True)


def split_kernel(place, mine, got, *outs):
    rows = outs[0].shape[0]
    for mask, out in enumerate(outs):
        here = pl.ds(pl.multiple_of((place[4] ^ mask) * rows, 16), rows)
        out[...] = (mine[here, :].astype(F32) + got[here, :].astype(F32)).astype(BF16)


def sum_rows(place, keep, send):
    got = swap(send, 1)
    span = keep.shape[0] // 2
    near = swap(add_two(keep[span:], got[span:]), 2)
    pieces = call(split_kernel, [shape(span // 4, keep.shape[1])] * 4, [place, add_two(keep[:span], got[:span]), near])
    total = add_two(pieces[0], *[level_swap(pieces[k], k) for k in (1, 2, 3)])
    return [total] + [level_swap(total, k) for k in (1, 2, 3)]


def finish_output(place, values, bias, *refs):
    pieces, out = refs[:-1], refs[-1]
    rows = pieces[0].shape[0]
    for mask, piece in enumerate(pieces):
        here = pl.ds(pl.multiple_of((place[4] ^ mask) * rows, 16), rows)
        out[here, :] = (values[here, :].astype(F32) + piece[...].astype(F32) + bias[...]).astype(BF16)


def finish_grad(place, values, grads, *refs):
    pieces, out = refs[:-1], refs[-1]
    rows = pieces[0].shape[0]
    for mask, piece in enumerate(pieces):
        here = pl.ds(pl.multiple_of((place[4] ^ mask) * rows, 16), rows)
        residual = values[here, :].astype(F32)
        centred = residual - jnp.mean(residual, axis=1, keepdims=True)
        scale = lax.rsqrt(jnp.mean(centred * centred, axis=1, keepdims=True) + EPSILON)
        normal = centred * scale
        total = piece[...].astype(F32)
        back = total - jnp.mean(total, axis=1, keepdims=True) - normal * jnp.mean(total * normal, axis=1, keepdims=True)
        out[here, :] = grads[here, :].astype(F32) + back * scale


def local(inputs, cotangent, piece_starts, positions, w_qkv, b_qkv, w_dense, w_fc1, b_fc1, w_fc2, out_bias,
          ln1_gain, ln1_bias, ln2_gain, ln2_bias):
    span, width = inputs.shape[1:]
    rows = w_fc1.shape[0]
    shards = lax.axis_size("shard")
    shard, ctx, level = lax.axis_index("shard"), lax.axis_index("ctx"), lax.axis_index("tensor")
    place = jnp.stack([ctx, ctx % 2, ctx // 2, shard, level])
    length = 4 * span
    quarter = w_fc1.shape[1] // 4
    joint = 2 * HEAD
    values, grads = inputs.reshape(span, width), cotangent.reshape(span, width)
    starts = piece_starts.reshape(-1)
    row = lambda vector: vector.reshape(1, -1)
    steps = range(1, shards)

    sent = call(prepare_joint, [shape(rows, joint)] * 4, [place, w_qkv.reshape(rows, -1), w_dense.reshape(rows, -1)])
    qd = [sent[0]] + [swap(sent[m], m) for m in (2, 3, 1)]
    qd = list(zip(qd, (0, 2, 3, 1)))

    def spread(block):
        size = span // 2
        return swap(lax.dynamic_slice(block, ((level % 2) * size, 0), (size, width)), 2)

    near_values = spread(values)
    near_grads = spread(grads)
    inner = [shape(2 * rows, quarter)] * 2 + [shape(rows, quarter)] * 4
    own, core, one_x, one_d, two_x, two_d = call(prepare_inner, inner, [place, w_fc1, w_fc2])
    core = swap(core, 1)
    one_x, one_d = swap(one_x, 2), swap(one_d, 3)
    two_x, two_d = swap(two_x, 2), swap(two_d, 3)

    joint_blocks = [(block, (0, m, 0)) for block, m in qd] + [(shift(block, -k), (0, m, k)) for block, m in qd for k in steps]
    both = [(own, 0, 0), (core, 1, 0)] + [(shift(own, -k), 0, k) for k in steps] + [(shift(core, -k), 1, k) for k in steps]

    def with_far(first, x, d):
        return ([(block, (first, m, k)) for block, m, k in both] + [(x, (0, 2, 0)), (d, (0, 3, 0))]
                + [(shift(x, -k), (0, 2, k)) for k in steps] + [(shift(d, -k), (0, 3, k)) for k in steps])

    one_blocks, two_blocks = with_far(0, one_x, one_d), with_far(rows, two_x, two_d)

    def all_tokens(block, near):
        far = level_swap(near, 1)
        return [block, near, far, swap(block, 1), swap(near, 1), swap(far, 1)]

    all_values = all_tokens(values, near_values)
    all_grads = all_tokens(grads, near_grads)
    gains = [row(ln1_gain), row(ln1_bias), row(ln2_gain), row(ln2_bias)]
    eighth = pl.BlockSpec((length // 8, width), lambda i, *_: (i, 0))
    normed_one, normed_two, plain = call(
        norm_kernel, [shape(length, width)] * 3, [place, *all_values, *gains], grid=(8,),
        in_specs=[whole(a) for a in all_values + gains], out_specs=[eighth] * 3)

    def blocked(array, count=4):
        return pl.BlockSpec((array.shape[0] // count, array.shape[1]), lambda i, *_: (i, 0))

    lanes = np.arange(HALF)
    frequency = np.where(lanes < ROT, ROPE_BASE ** (-(lanes % (ROT // 2)) * 2.0 / ROT), 0.0).astype(np.float32)[None]
    bias = row(b_qkv.reshape(-1))
    blocks = [block for block, _ in joint_blocks]
    table = shape(length, HALF, kind=F32)
    outs = [shape(length, HEAD + HALF), table, table, shape(width, joint)]
    mine, cosine, sine, w_joint = call(
        functools.partial(joint_kernel, rows, shards, [p for _, p in joint_blocks]), outs,
        [place, starts, normed_one, bias, jnp.asarray(frequency), *blocks], flops=2 * length * width * (HEAD + HALF), grid=(4,), prefetch=1,
        in_specs=[blocked(normed_one), whole(bias), whole(frequency)] + [whole(b) for b in blocks],
        out_specs=[blocked(o) for o in outs[:3]] + [whole(outs[3])])
    outs = [shape(length, HALF), shape(length, width), shape(1, width, kind=F32)]
    grad_mine, grads_full, grad_total = call(
        context_kernel, outs, [place, *all_grads, w_joint], flops=2 * length * width * HALF, grid=(8,),
        in_specs=[whole(a) for a in all_grads + [w_joint]], out_specs=[blocked(outs[0], 8), blocked(outs[1], 8), whole(outs[2])])
    context, grad_joined = call(
        attention_kernel, [shape(length, HALF), shape(length, HEAD + HALF)],
        [place, starts, mine, swap(mine, 1), grad_mine, swap(grad_mine, 1), cosine, sine], prefetch=1, flops=8 * length * length * HEAD,
        scratch=[pltpu.VMEM((length, HEAD), BF16)] * 4 + [pltpu.VMEM((length, HEAD), F32), pltpu.VMEM((length, HALF), F32)])

    bias = row(b_fc1)
    blocks = [block for block, _ in one_blocks]
    outs = [shape(length, quarter), shape(length, quarter, kind=F32), shape(width, quarter)]
    hidden, slope, fc1 = call(
        functools.partial(hidden_kernel, rows, shards, [p for _, p in one_blocks]), outs, [place, normed_two, bias, *blocks],
        flops=2 * length * width * quarter, grid=(4,), in_specs=[blocked(normed_two), whole(bias)] + [whole(b) for b in blocks],
        out_specs=[blocked(o) for o in outs[:2]] + [whole(outs[2])])
    fc2_parts = weight_grad(place, [grads_full], [hidden], rows, shards)
    qd_parts = weight_grad(place, [normed_one, grads_full], [grad_joined, context], rows, shards)
    blocks = [block for block, _ in two_blocks]
    outs = [shape(length, quarter), shape(width, quarter)]
    grad_inner, fc2 = call(
        functools.partial(inner_kernel, rows, shards, [p for _, p in two_blocks]), outs, [place, grads_full, slope, *blocks],
        flops=2 * length * width * quarter, grid=(4,), in_specs=[blocked(grads_full), blocked(slope)] + [whole(b) for b in blocks],
        out_specs=[blocked(outs[0]), whole(outs[1])])
    fc1_parts = weight_grad(place, [normed_two], [grad_inner], rows, shards)

    first_half = pl.BlockSpec((span, width), lambda i, *_: (jnp.minimum(i, 1), 0))
    second_half = pl.BlockSpec((span, width), lambda i, *_: (jnp.maximum(i - 2, 0), 0))
    args = [grad_joined, grad_inner, w_joint, fc1, gains[0], gains[2], plain, grad_total]
    keep, send, small = call(
        back_kernel, [shape(2 * span, width)] * 2 + [shape(8, width, kind=F32)], [place, *args], flops=2 * length * width * (HEAD + HALF + quarter), grid=(4,),
        in_specs=[blocked(args[0]), blocked(args[1])] + [whole(a) for a in args[2:6]] + [blocked(plain), whole(grad_total)],
        out_specs=[first_half, second_half, pl.BlockSpec((8, width), lambda *_: (0, 0))])
    pieces = sum_rows(place, keep, send)
    grad_inputs, = call(finish_grad, [shape(span, width, kind=F32)], [place, values, grads, *pieces])

    args = [context, hidden, w_joint, fc2]
    keep, send = call(
        output_kernel, [shape(2 * span, width)] * 2, [place, *args], flops=2 * length * width * (HALF + quarter), grid=(4,),
        in_specs=[blocked(context), blocked(hidden), whole(w_joint), whole(fc2)], out_specs=[first_half, second_half])
    pieces = sum_rows(place, keep, send)
    output, = call(finish_output, [shape(span, width)], [place, values, row(out_bias), *pieces])

    small = small + swap(small, 1)
    small = small + swap(small, 2)
    front = small[:4]
    front = front + level_swap(front, 1)
    front = front + level_swap(front, 2)
    small = jnp.concatenate([front, small[4:]])
    step = 1
    while step < shards:
        small = small + lax.ppermute(small, "shard", [(i, i ^ step) for i in range(shards)])
        step *= 2

    grad_w_fc2, = call(place_inner, [shape(rows, 4 * quarter, kind=F32)], [place, *reduce_weight(*fc2_parts, rows, shards)])
    grad_w_qkv, grad_w_dense = call(place_joint, [shape(rows, 6 * HEAD, kind=F32), shape(rows, 2 * HEAD, kind=F32)],
                                    [place, *reduce_weight(*qd_parts, rows, shards)])
    grad_w_fc1, = call(place_inner, [shape(rows, 4 * quarter, kind=F32)], [place, *reduce_weight(*fc1_parts, rows, shards)])
    return (
        output[None],
        grad_inputs[None],
        grad_w_qkv.reshape(w_qkv.shape),
        small[5, :b_qkv.size].reshape(b_qkv.shape),
        grad_w_dense.reshape(w_dense.shape),
        grad_w_fc1,
        small[6, :b_fc1.size],
        grad_w_fc2,
        small[4],
        small[0],
        small[1],
        small[2],
        small[3],
    )


def solution(mesh):
    rows = P(("shard", "ctx"), "tensor")
    tokens = P("shard", "ctx", None)
    heads = P(("shard", "ctx"), "tensor", None)
    in_specs = (tokens, tokens, P("shard", None), P("shard", "ctx"), heads, P("tensor", None), heads, rows, P("tensor"), rows,
                P(), P(), P(), P(), P())
    out_specs = (tokens, tokens, heads, P("tensor", None), heads, rows, P("tensor"), rows, P(), P(), P(), P(), P())
    return jax.shard_map(local, mesh=mesh, in_specs=in_specs, out_specs=out_specs, check_vma=False)
```

time: 883 us -> 393 us (0.45)
  waiting for transfers between devices: 666 us -> 164 us
  Pallas kernels: 0 us -> 89.7 us
  starting transfers between devices: 1.39 us -> 78.7 us
  matrix products: 67.5 us -> 0 us
  other arithmetic: 51.4 us -> 9.83 us
  blocking collectives: 25.1 us -> 0 us
  between operations: 14.9 us -> 1.63 us
    reduce_scatter x4 -> x0, waiting for transfers between devices: 316 us -> none  [the longest x1 178 us: local(): lax.psum_scatter(jnp.concatenate([outer_rows(normed_one, grad_joined), ou...]
    psum x1 -> x0, waiting for transfers between devices: 184 us -> none  [local(): summed_out = lax.psum(block_out, 'tensor')]
    all_gather x6 -> x0, waiting for transfers between devices: 165 us -> none  [the longest x1 49.6 us: local(): lax.all_gather(fc2_low, ('shard', 'ctx'), axis=0, tiled=True)]
    ppermute x0 -> x66, waiting for transfers between devices: none -> 164 us  [the longest x16 62.3 us: shift(): lax.ppermute(value, 'shard', [(i, (i + step) % size) for i in range(size)])]
    pallas_call x0 -> x20, Pallas kernels: none -> 89.7 us  [call(): pl.pallas_call(kernel, out_shape=outs, compiler_params=pltpu.CompilerPara...]
    ppermute x0 -> x66, starting transfers between devices: none -> 78.7 us  [the longest x16 41.3 us: level_swap(): return lax.ppermute(value, 'tensor', [(i, i ^ mask) for i in range(4)])]
    dot_general x18 -> x0, matrix products: 67.5 us -> none  [the longest x4 22.4 us: cross_rows(): lax.dot_general(left_rows, right_rows, (((1,), (1,)), ((), ())), preferre...]
    concatenate x5 -> x1, other arithmetic: 26 us -> 0.02 us  [local(): small = jnp.concatenate([front, small[4:]])]
  transfers between devices with their start and end apart: 11 -> 66, of which waited for: 11 -> 24; matrix products, arithmetic and copies ran while one was open for 16% -> 4% of each run, Pallas kernels for 0% -> 17%
where the time goes in v1:
time: 393 us; the launch traced here: 390 us
  waiting for transfers between devices  164 us (42%)
  Pallas kernels  89.7 us (23%)
  starting transfers between devices  78.7 us (20%)
  local copies, waits for them, and re-layouts  45.4 us (12%)
  other arithmetic  9.83 us (3%)
    pallas_call x20, Pallas kernels, call(): pl.pallas_call(kernel, out_shape=outs, compiler_params=pltpu.CompilerPara...  89.7 us
    ppermute x16, waiting for transfers between devices, shift(): lax.ppermute(value, 'shard', [(i, (i + step) % size) for i in range(size)])  62.3 us
    ppermute x33, waiting for transfers between devices, swap(): return lax.ppermute(value, 'ctx', [(i, i ^ mask) for i in range(4)])  61.9 us
    ppermute x16, starting transfers between devices, level_swap(): return lax.ppermute(value, 'tensor', [(i, i ^ mask) for i in range(4)])  41.3 us
    ppermute x16, waiting for transfers between devices, level_swap(): return lax.ppermute(value, 'tensor', [(i, i ^ mask) for i in range(4)])  40.2 us
    unnamed x147, local copies, waits for them, and re-layouts  39.7 us
    ppermute x33, starting transfers between devices, swap(): return lax.ppermute(value, 'ctx', [(i, i ^ mask) for i in range(4)])  19 us
    ppermute x16, starting transfers between devices, shift(): lax.ppermute(value, 'shard', [(i, (i + step) % size) for i in range(size)])  17.9 us
  transfers between devices with their start and end apart: 66, of which 24 were waited for; matrix products, arithmetic and copies ran while one was open for 4% of the time, Pallas kernels for 17%

profile of v1, /device:TPU:0, one launch (start us, length us, event | category | flops | bytes accessed | tf_op | source)
XLA Modules:
  0.0 389.8 jit_solution(92953865194861993)
XLA Ops:
  1.8 1.6 copy.29
  5.7 2.9 collective-permute-start.5
  16.1 1.9 collective-permute-start.22
  18.1 3.2 collective-permute-done.6.refs_2_
  21.4 1.7 collective-permute-start.23
  23.1 1.7 collective-permute-start.26
  24.8 13.6 %collective-permute-done.22.refs_4_ = bf16[256,512]{1,0:T(8,128)(2,1)S(1)} collective-permute-done((bf16[256,512]{1,0:T(8,128)(2,1)S(1)}, bf16[256,512]{1,0:T(8,128)(2,1)S(1)}, u32[]{:S(2)}, u32[]{:S(2)}) %collective-permute-start.22) | collective-permute-done | bytes 262176 | tf_op jit(solution)/shard_map/ppermute | solution.py:52
  38.5 16.4 %collective-permute-done.23.refs_5_ = bf16[256,512]{1,0:T(8,128)(2,1)S(1)} collective-permute-done((bf16[256,512]{1,0:T(8,128)(2,1)S(1)}, bf16[256,512]{1,0:T(8,128)(2,1)S(1)}, u32[]{:S(2)}, u32[]{:S(2)}) %collective-permute-start.23) | collective-permute-done | bytes 262176 | tf_op jit(solution)/shard_map/ppermute | solution.py:52
  55.1 5.9 %collective-permute-done.26.refs_4_ = bf16[256,512]{1,0:T(8,128)(2,1)} collective-permute-done((bf16[256,512]{1,0:T(8,128)(2,1)S(1)}, bf16[256,512]{1,0:T(8,128)(2,1)}, u32[]{:S(2)}, u32[]{:S(2)}) %collective-permute-start.26) | collective-permute-done | bytes 262176 | tf_op jit(solution)/shard_map/ppermute | solution.py:52
  61.0 2.1 collective-permute-start.9
  63.1 1.9 collective-permute-done.27.refs_5_
  69.8 4.4 %collective-permute-done.10.refs_6_ = bf16[256,512]{1,0:T(8,128)(2,1)S(1)} collective-permute-done((bf16[256,512]{1,0:T(8,128)(2,1)S(1)}, bf16[256,512]{1,0:T(8,128)(2,1)S(1)}, u32[]{:S(2)}, u32[]{:S(2)}) %collective-permute-start.10) | collective-permute-done | bytes 262176 | tf_op jit(solution)/shard_map/ppermute | solution.py:61
  74.2 5.5 %collective-permute-done.11.refs_7_ = bf16[256,512]{1,0:T(8,128)(2,1)S(1)} collective-permute-done((bf16[256,512]{1,0:T(8,128)(2,1)S(1)}, bf16[256,512]{1,0:T(8,128)(2,1)S(1)}, u32[]{:S(2)}, u32[]{:S(2)}) %collective-permute-start.11) | collective-permute-done | bytes 262176 | tf_op jit(solution)/shard_map/ppermute | solution.py:61
  81.9 6.0 %collective-permute-done.24.refs_6_ = bf16[256,512]{1,0:T(8,128)(2,1)S(1)} collective-permute-done((bf16[256,512]{1,0:T(8,128)(2,1)S(1)}, bf16[256,512]{1,0:T(8,128)(2,1)S(1)}, u32[]{:S(2)}, u32[]{:S(2)}) %collective-permute-start.24) | collective-permute-done | bytes 262176 | tf_op jit(solution)/shard_map/ppermute | solution.py:61
  89.1 4.0 %collective-permute-done.14.far = bf16[128,2048]{1,0:T(8,128)(2,1)S(1)} collective-permute-done((bf16[128,2048]{1,0:T(8,128)(2,1)S(1)}, bf16[128,2048]{1,0:T(8,128)(2,1)S(1)}, u32[]{:S(2)}, u32[]{:S(2)}) %collective-permute-start.14) | collective-permute-done | bytes 524320 | tf_op jit(solution)/shard_map/ppermute | solution.py:56
  93.7 1.7 collective-permute-start.25
  96.2 7.3 %shard_map.246 = (bf16[1024,2048]{1,0:T(8,128)(2,1)S(1)}, bf16[1024,2048]{1,0:T(8,128)(2,1)S(1)}, bf16[1024,2048]{1,0:T(8,128)(2,1)}) custom-call(s32[5]{0:T(128)S(1)} %stack.23.place, bf16[256,2048]{1,0:T(8,128)(2,1)S(1)} %bitcast.40, bf16[128,2048]{1,0:T(8,128)(2,1)S(1)} %collective-permute-done.near, bf16[128,2048]{1,0:T(8,128)(2,1)S(1)} %collective-permute-done.1.far, ...), custom_call_target="tpu_custom_call" | custom-call | bytes 16810004 | tf_op jit(solution)/shard_map/pallas_call | solution.py:41
  103.5 2.0 copy-done.42
  106.6 1.7 collective-permute-start.21
  108.3 6.5 %shard_map.248 = (bf16[1024,384]{1,0:T(8,128)(2,1)S(1)}, f32[1024,128]{1,0:T(8,128)S(1)}, f32[1024,128]{1,0:T(8,128)S(1)}, bf16[2048,512]{1,0:T(8,128)(2,1)S(1)}) custom-call(s32[5]{0:T(128)S(1)} %stack.23.place, s32[3]{0:T(128)S(1)} %bitcast.56, bf16[1024,2048]{1,0:T(8,128)(2,1)S(1)} %get-tuple-element.64.normed.refs_0_, f32[1,1536]{1,0:T(1,128)S(1)} %bitcast.48, ...), custom_call_target="tpu_custom_call" | custom-call | flops 1610612736 | bytes 10230304 | tf_op jit(solution)/shard_map/pallas_call | solution.py:41
  118.6 1.7 collective-permute-start.29
  121.4 4.8 %shard_map.249 = (bf16[1024,128]{1,0:T(8,128)(2,1)}, bf16[1024,2048]{1,0:T(8,128)(2,1)S(1)}, f32[1,2048]{1,0:T(1,128)S(1)}) custom-call(s32[5]{0:T(128)S(1)} %stack.23.place, bf16[256,2048]{1,0:T(8,128)(2,1)S(1)} %bitcast.44, bf16[128,2048]{1,0:T(8,128)(2,1)S(1)} %collective-permute-done.13.near, bf16[128,2048]{1,0:T(8,128)(2,1)S(1)} %collective-permute-done.14.far, ...), custom_call_target="tpu_custom_call" | custom-call | flops 536870912 | bytes 10756116 | tf_op jit(solution)/shard_map/pallas_call | solution.py:41
  127.0 5.2 %collective-permute-done.21.refs_3_ = bf16[512,512]{1,0:T(8,128)(2,1)S(1)} collective-permute-done((bf16[512,512]{1,0:T(8,128)(2,1)S(1)}, bf16[512,512]{1,0:T(8,128)(2,1)S(1)}, u32[]{:S(2)}, u32[]{:S(2)}) %collective-permute-start.21) | collective-permute-done | bytes 524320 | tf_op jit(solution)/shard_map/ppermute | solution.py:61
  135.1 2.2 copy-done.43
  137.3 4.3 %shard_map.252 = (bf16[1024,512]{1,0:T(8,128)(2,1)S(1)}, f32[1024,512]{1,0:T(8,128)S(1)}, bf16[2048,512]{1,0:T(8,128)(2,1)S(1)}) custom-call(s32[5]{0:T(128)S(1)} %stack.23.place, bf16[1024,2048]{1,0:T(8,128)(2,1)S(1)} %copy-done.43, f32[1,2048]{1,0:T(1,128)S(1)} %bitcast.62, bf16[512,512]{1,0:T(8,128)(2,1)S(1)} %get-tuple-element.76.refs_0_, ...), custom_call_target="tpu_custom_call" | custom-call | flops 2147483648 | bytes 12591124 | tf_op jit(solution)/shard_map/pallas_call | solution.py:41
  146.8 4.6 %shard_map.253 = (bf16[1024,512]{1,0:T(8,128)(2,1)S(1)}, bf16[2048,512]{1,0:T(8,128)(2,1)S(1)}) custom-call(s32[5]{0:T(128)S(1)} %stack.23.place, bf16[1024,2048]{1,0:T(8,128)(2,1)S(1)} %get-tuple-element.81.grads.refs_1_.refs_0_, f32[1024,512]{1,0:T(8,128)S(1)} %copy-done.10, bf16[512,512]{1,0:T(8,128)(2,1)S(1)} %get-tuple-element.76.refs_0_, ...), custom_call_target="tpu_custom_call" | custom-call | flops 2147483648 | bytes 12582932 | tf_op jit(solution)/shard_map/pallas_call | solution.py:41
  151.5 10.3 %shard_map.250 = (bf16[1024,128]{1,0:T(8,128)(2,1)S(1)}, bf16[1024,384]{1,0:T(8,128)(2,1)S(1)}) custom-call(s32[5]{0:T(128)S(1)} %stack.23.place, s32[3]{0:T(128)S(1)} %bitcast.57, bf16[1024,384]{1,0:T(8,128)(2,1)S(1)} %copy-done.51, bf16[1024,384]{1,0:T(8,128)(2,1)} %collective-permute-done.12.got, bf16[1024,128]{1,0:T(8,128)(2,1)} %get-tuple-element.71.grad_mine, ...), custom_call_target="tpu_custom_call" | custom-call | flops 2147483648 | bytes 4194336 | tf_op jit(solution)/shard_map/pallas_call | solution.py:41
  162.5 2.5 copy-done.45
  165.0 10.4 %shard_map.257 = (bf16[512,2048]{1,0:T(8,128)(2,1)S(1)}, bf16[512,2048]{1,0:T(8,128)(2,1)}, f32[8,2048]{1,0:T(8,128)S(1)}) custom-call(s32[5]{0:T(128)S(1)} %stack.23.place, bf16[1024,384]{1,0:T(8,128)(2,1)S(1)} %get-tuple-element.92.grad.refs_2_, bf16[1024,512]{1,0:T(8,128)(2,1)S(1)} %get-tuple-element.93.inner.refs_1_, bf16[2048,512]{1,0:T(8,128)(2,1)S(1)} %copy-done.7, ...), custom_call_target="tpu_custom_call" | custom-call | flops 3758096384 | bytes 14508052 | tf_op jit(solution)/shard_map/pallas_call | solution.py:41
  182.1 6.0 %shard_map.254 = (bf16[512,2048]{1,0:T(8,128)(2,1)S(1)}, bf16[512,2048]{1,0:T(8,128)(2,1)}) custom-call(s32[5]{0:T(128)S(1)} %stack.23.place, bf16[1024,128]{1,0:T(8,128)(2,1)S(1)} %copy-done.31, bf16[1024,512]{1,0:T(8,128)(2,1)S(1)} %copy-done.69, bf16[2048,512]{1,0:T(8,128)(2,1)S(1)} %copy-done.8, bf16[2048,512]{1,0:T(8,128)(2,1)S(1)} %copy-done.47), custom_call_target="tpu_custom_call" | custom-call | flops 2684354560 | bytes 9699348 | tf_op jit(solution)/shard_map/pallas_call | solution.py:41
  188.6 5.3 %shard_map.264 = (bf16[1,512,512]{2,1,0:T(8,128)(2,1)S(1)}, bf16[1,512,512]{2,1,0:T(8,128)(2,1)S(1)}, bf16[1024,512]{1,0:T(8,128)(2,1)S(1)}) custom-call(s32[5]{0:T(128)S(1)} %stack.23.place, bf16[1024,2048]{1,0:T(8,128)(2,1)S(1)} %get-tuple-element.81.grads.refs_1_.refs_0_, bf16[1024,512]{1,0:T(8,128)(2,1)S(1)} %copy-done.70), custom_call_target="tpu_custom_call" | custom-call | flops 2147483648 | bytes 7340052 | tf_op jit(solution)/shard_map/pallas_call | solution.py:41
  194.4 1.7 collective-permute-start.63
  198.9 5.3 %shard_map.262 = (bf16[1,512,512]{2,1,0:T(8,128)(2,1)S(1)}, bf16[1,512,512]{2,1,0:T(8,128)(2,1)S(1)}, bf16[1024,512]{1,0:T(8,128)(2,1)S(1)}) custom-call(s32[5]{0:T(128)S(1)} %stack.23.place, bf16[1024,2048]{1,0:T(8,128)(2,1)S(1)} %copy-done.44, bf16[1024,512]{1,0:T(8,128)(2,1)S(1)} %copy-done.49), custom_call_target="tpu_custom_call" | custom-call | flops 2147483648 | bytes 7340052 | tf_op jit(solution)/shard_map/pallas_call | solution.py:41
  204.8 4.0 %collective-permute-done.61 = bf16[512,512]{1,0:T(8,128)(2,1)S(1)} collective-permute-done((bf16[512,512]{1,0:T(8,128)(2,1)S(1)}, bf16[512,512]{1,0:T(8,128)(2,1)S(1)}, u32[]{:S(2)}, u32[]{:S(2)}) %collective-permute-start.61) | collective-permute-done | bytes 524320 | tf_op jit(solution)/shard_map/ppermute | solution.py:61
  209.2 10.9 %collective-permute-done.63 = bf16[512,512]{1,0:T(8,128)(2,1)S(1)} collective-permute-done((bf16[512,512]{1,0:T(8,128)(2,1)S(1)}, bf16[512,512]{1,0:T(8,128)(2,1)S(1)}, u32[]{:S(2)}, u32[]{:S(2)}) %collective-permute-start.63) | collective-permute-done | bytes 524320 | tf_op jit(solution)/shard_map/ppermute | solution.py:61
  222.0 2.0 collective-permute-done.53
  224.0 7.3 %collective-permute-done.56 = bf16[512,512]{1,0:T(8,128)(2,1)S(1)} collective-permute-done((bf16[512,512]{1,0:T(8,128)(2,1)S(1)}, bf16[512,512]{1,0:T(8,128)(2,1)S(1)}, u32[]{:S(2)}, u32[]{:S(2)}) %collective-permute-start.56) | collective-permute-done | bytes 524320 | tf_op jit(solution)/shard_map/ppermute | solution.py:61
  231.3 2.6 collective-permute-start.54
  233.9 7.7 %collective-permute-done.58 = bf16[512,512]{1,0:T(8,128)(2,1)S(1)} collective-permute-done((bf16[512,512]{1,0:T(8,128)(2,1)S(1)}, bf16[512,512]{1,0:T(8,128)(2,1)S(1)}, u32[]{:S(2)}, u32[]{:S(2)}) %collective-permute-start.58) | collective-permute-done | bytes 524320 | tf_op jit(solution)/shard_map/ppermute | solution.py:61
  243.9 3.6 add_convert_fusion
  249.0 3.7 add_convert_fusion.2
  253.3 2.9 collective-permute-done.59.refs_2_
  257.0 8.6 %shard_map.260 = (bf16[1,512,512]{2,1,0:T(8,128)(2,1)}, bf16[1,512,512]{2,1,0:T(8,128)(2,1)}, bf16[1024,512]{1,0:T(8,128)(2,1)S(1)}) custom-call(s32[5]{0:T(128)S(1)} %stack.23.place, bf16[1024,2048]{1,0:T(8,128)(2,1)S(1)} %get-tuple-element.64.normed.refs_0_, bf16[1024,2048]{1,0:T(8,128)(2,1)S(1)} %get-tuple-element.81.grads.refs_1_.refs_0_, ...), custom_call_target="tpu_custom_call" | custom-call | flops 2147483648 | bytes 11534356 | tf_op jit(solution)/shard_map/pallas_call | solution.py:41
  265.6 2.0 shard_map.263
  267.6 16.7 %collective-permute-done.64.refs_2_ = bf16[256,512]{1,0:T(8,128)(2,1)S(1)} collective-permute-done((bf16[256,512]{1,0:T(8,128)(2,1)S(1)}, bf16[256,512]{1,0:T(8,128)(2,1)S(1)}, u32[]{:S(2)}, u32[]{:S(2)}) %collective-permute-start.64) | collective-permute-done | bytes 262176 | tf_op jit(solution)/shard_map/ppermute | solution.py:52
  286.3 2.0 shard_map.265
  290.6 1.6 collective-permute-start.40
  292.2 2.6 collective-permute-start.41
  294.8 4.6 %collective-permute-done.46 = bf16[512,512]{1,0:T(8,128)(2,1)} collective-permute-done((bf16[512,512]{1,0:T(8,128)(2,1)}, bf16[512,512]{1,0:T(8,128)(2,1)}, u32[]{:S(2)}, u32[]{:S(2)}) %collective-permute-start.46) | collective-permute-done | bytes 524320 | tf_op jit(solution)/shard_map/ppermute | solution.py:61
  299.4 3.6 collective-permute-start.42
  303.0 6.7 %collective-permute-done.48 = bf16[512,512]{1,0:T(8,128)(2,1)} collective-permute-done((bf16[512,512]{1,0:T(8,128)(2,1)}, bf16[512,512]{1,0:T(8,128)(2,1)}, u32[]{:S(2)}, u32[]{:S(2)}) %collective-permute-start.48) | collective-permute-done | bytes 524320 | tf_op jit(solution)/shard_map/ppermute | solution.py:61
  313.6 1.6 collective-permute-start.32
  315.2 2.6 collective-permute-start.33
  318.2 10.0 %collective-permute-done.32 = bf16[64,2048]{1,0:T(8,128)(2,1)S(1)} collective-permute-done((bf16[64,2048]{1,0:T(8,128)(2,1)S(1)}, bf16[64,2048]{1,0:T(8,128)(2,1)S(1)}, u32[]{:S(2)}, u32[]{:S(2)}) %collective-permute-start.32) | collective-permute-done | bytes 262176 | tf_op jit(solution)/shard_map/ppermute | solution.py:56
  328.4 8.2 %collective-permute-done.33 = bf16[64,2048]{1,0:T(8,128)(2,1)S(1)} collective-permute-done((bf16[64,2048]{1,0:T(8,128)(2,1)S(1)}, bf16[64,2048]{1,0:T(8,128)(2,1)S(1)}, u32[]{:S(2)}, u32[]{:S(2)}) %collective-permute-start.33) | collective-permute-done | bytes 262176 | tf_op jit(solution)/shard_map/ppermute | solution.py:56
  336.6 2.5 collective-permute-start.45
  339.1 10.3 %collective-permute-start.44 = (bf16[64,2048]{1,0:T(8,128)(2,1)S(1)}, bf16[64,2048]{1,0:T(8,128)(2,1)}, u32[]{:S(2)}, u32[]{:S(2)}) collective-permute-start(bf16[64,2048]{1,0:T(8,128)(2,1)S(1)} %add_convert_fusion.16.refs_0_), channel_id=1, source_target_pairs={{0,2},{1,3},{2,0},{3,1},{4,6},{5,7},{6,4},{7,5},{8,10},{9,11},{10,... | collective-permute-start | bytes 786440 | tf_op jit(solution)/shard_map/ppermute | solution.py:56
  351.1 2.0 collective-permute-start.36
  353.1 6.5 %collective-permute-start.35 = (bf16[64,2048]{1,0:T(8,128)(2,1)S(1)}, bf16[64,2048]{1,0:T(8,128)(2,1)}, u32[]{:S(2)}, u32[]{:S(2)}) collective-permute-start(bf16[64,2048]{1,0:T(8,128)(2,1)S(1)} %add_convert_fusion.17.refs_0_), channel_id=1, source_target_pairs={{0,1},{1,0},{2,3},{3,2},{4,5},{5,4},{6,7},{7,6},{8,9},{9,8},{10,11... | collective-permute-start | bytes 786440 | tf_op jit(solution)/shard_map/ppermute | solution.py:56
  362.2 3.1 reshape.78
  366.4 9.7 %collective-permute-done.44.refs_2_ = bf16[64,2048]{1,0:T(8,128)(2,1)} collective-permute-done((bf16[64,2048]{1,0:T(8,128)(2,1)S(1)}, bf16[64,2048]{1,0:T(8,128)(2,1)}, u32[]{:S(2)}, u32[]{:S(2)}) %collective-permute-start.44) | collective-permute-done | bytes 262176 | tf_op jit(solution)/shard_map/ppermute | solution.py:56
  377.0 3.8 shard_map.259
  380.9 6.2 %collective-permute-done.36.refs_2_ = bf16[64,2048]{1,0:T(8,128)(2,1)} collective-permute-done((bf16[64,2048]{1,0:T(8,128)(2,1)S(1)}, bf16[64,2048]{1,0:T(8,128)(2,1)}, u32[]{:S(2)}, u32[]{:S(2)}) %collective-permute-start.36) | collective-permute-done | bytes 262176 | tf_op jit(solution)/shard_map/ppermute | solution.py:56
  387.1 2.4 shard_map.256
  (257 shorter events, 69.6 us)
Async XLA Ops:
  5.7 10.4 %collective-permute-start.5 = (bf16[256,512]{1,0:T(8,128)(2,1)}, bf16[256,512]{1,0:T(8,128)(2,1)S(1)}, u32[]{:S(2)}, u32[]{:S(2)}) collective-permute-start(bf16[256,512]{1,0:T(8,128)(2,1)} %get-tuple-element.66), channel_id=1, source_target_pairs={{0,8},{4,12},{8,0},{12,4},{1,9},{5,13},{9,1},{13,5},{2,10},{6,14},... | collective-permute-start | bytes 786440 | tf_op jit(solution)/shard_map/ppermute | solution.py:52
  8.6 12.6 %collective-permute-start.6 = (bf16[256,512]{1,0:T(8,128)(2,1)}, bf16[256,512]{1,0:T(8,128)(2,1)S(1)}, u32[]{:S(2)}, u32[]{:S(2)}) collective-permute-start(bf16[256,512]{1,0:T(8,128)(2,1)} %get-tuple-element.67), channel_id=1, source_target_pairs={{0,12},{4,8},{8,4},{12,0},{1,13},{5,9},{9,5},{13,1},{2,14},{6,10},... | collective-permute-start | bytes 786440 | tf_op jit(solution)/shard_map/ppermute | solution.py:52
  8.7 58.5 %collective-permute-start.13 = (bf16[128,2048]{1,0:T(8,128)(2,1)S(1)}, bf16[128,2048]{1,0:T(8,128)(2,1)S(1)}, u32[]{:S(2)}, u32[]{:S(2)}) collective-permute-start(bf16[128,2048]{1,0:T(8,128)(2,1)S(1)} %dynamic-slice_bitcast_fusion), channel_id=1, source_target_pairs={{0,8},{4,12},{8,0},{12,4},{1,9},{5,13},{9,1},{13,5},{2,10},{6,14},... | collective-permute-start | bytes 1572872 | tf_op jit(solution)/shard_map/ppermute | solution.py:52
  10.0 11.5 %collective-permute-start.7 = (bf16[256,512]{1,0:T(8,128)(2,1)}, bf16[256,512]{1,0:T(8,128)(2,1)S(1)}, u32[]{:S(2)}, u32[]{:S(2)}) collective-permute-start(bf16[256,512]{1,0:T(8,128)(2,1)} %copy-done.64), channel_id=1, source_target_pairs={{0,4},{4,0},{8,12},{12,8},{1,5},{5,1},{9,13},{13,9},{2,6},{6,2},{1... | collective-permute-start | bytes 786440 | tf_op jit(solution)/shard_map/ppermute | solution.py:52
  10.6 12.5 %collective-permute-start.8 = (bf16[256,512]{1,0:T(8,128)(2,1)}, bf16[256,512]{1,0:T(8,128)(2,1)S(1)}, u32[]{:S(2)}, u32[]{:S(2)}) collective-permute-start(bf16[256,512]{1,0:T(8,128)(2,1)} %copy-done.24), channel_id=1, source_target_pairs={{0,16},{16,0},{1,17},{17,1},{2,18},{18,2},{3,19},{19,3},{4,20},{20... | collective-permute-start | bytes 786440 | tf_op jit(solution)/shard_map/ppermute | solution.py:61
  16.1 22.3 %collective-permute-start.22 = (bf16[256,512]{1,0:T(8,128)(2,1)S(1)}, bf16[256,512]{1,0:T(8,128)(2,1)S(1)}, u32[]{:S(2)}, u32[]{:S(2)}) collective-permute-start(bf16[256,512]{1,0:T(8,128)(2,1)S(1)} %get-tuple-element.78), channel_id=1, source_target_pairs={{0,8},{4,12},{8,0},{12,4},{1,9},{5,13},{9,1},{13,5},{2,10},{6,14},... | collective-permute-start | bytes 786440 | tf_op jit(solution)/shard_map/ppermute | solution.py:52
  21.3 46.5 %collective-permute-start = (bf16[128,2048]{1,0:T(8,128)(2,1)S(1)}, bf16[128,2048]{1,0:T(8,128)(2,1)S(1)}, u32[]{:S(2)}, u32[]{:S(2)}) collective-permute-start(bf16[128,2048]{1,0:T(8,128)(2,1)S(1)} %dynamic-slice_bitcast_fusion.1), channel_id=1, source_target_pairs={{0,8},{4,12},{8,0},{12,4},{1,9},{5,13},{9,1},{13,5},{2,10},{6,14},... | collective-permute-start | bytes 1572872 | tf_op jit(solution)/shard_map/ppermute | solution.py:52
  21.4 33.5 %collective-permute-start.23 = (bf16[256,512]{1,0:T(8,128)(2,1)S(1)}, bf16[256,512]{1,0:T(8,128)(2,1)S(1)}, u32[]{:S(2)}, u32[]{:S(2)}) collective-permute-start(bf16[256,512]{1,0:T(8,128)(2,1)S(1)} %get-tuple-element.79), channel_id=1, source_target_pairs={{0,12},{4,8},{8,4},{12,0},{1,13},{5,9},{9,5},{13,1},{2,14},{6,10},... | collective-permute-start | bytes 786440 | tf_op jit(solution)/shard_map/ppermute | solution.py:52
  23.1 37.9 %collective-permute-start.26 = (bf16[256,512]{1,0:T(8,128)(2,1)S(1)}, bf16[256,512]{1,0:T(8,128)(2,1)}, u32[]{:S(2)}, u32[]{:S(2)}) collective-permute-start(bf16[256,512]{1,0:T(8,128)(2,1)S(1)} %get-tuple-element.83), channel_id=1, source_target_pairs={{0,8},{4,12},{8,0},{12,4},{1,9},{5,13},{9,1},{13,5},{2,10},{6,14},... | collective-permute-start | bytes 786440 | tf_op jit(solution)/shard_map/ppermute | solution.py:52
  38.5 26.6 %collective-permute-start.27 = (bf16[256,512]{1,0:T(8,128)(2,1)S(1)}, bf16[256,512]{1,0:T(8,128)(2,1)}, u32[]{:S(2)}, u32[]{:S(2)}) collective-permute-start(bf16[256,512]{1,0:T(8,128)(2,1)S(1)} %get-tuple-element.84), channel_id=1, source_target_pairs={{0,12},{4,8},{8,4},{12,0},{1,13},{5,9},{9,5},{13,1},{2,14},{6,10},... | collective-permute-start | bytes 786440 | tf_op jit(solution)/shard_map/ppermute | solution.py:52
  54.9 38.8 %collective-permute-start.2 = (bf16[256,2048]{1,0:T(8,128)(2,1)S(1)}, bf16[256,2048]{1,0:T(8,128)(2,1)S(1)}, u32[]{:S(2)}, u32[]{:S(2)}) collective-permute-start(bf16[256,2048]{1,0:T(8,128)(2,1)S(1)} %bitcast.39), channel_id=1, source_target_pairs={{0,4},{4,0},{8,12},{12,8},{1,5},{5,1},{9,13},{13,9},{2,6},{6,2},{1... | collective-permute-start | bytes 3145736 | tf_op jit(solution)/shard_map/ppermute | solution.py:52
  61.0 8.3 %collective-permute-start.9 = (bf16[256,512]{1,0:T(8,128)(2,1)S(1)}, bf16[256,512]{1,0:T(8,128)(2,1)S(1)}, u32[]{:S(2)}, u32[]{:S(2)}) collective-permute-start(bf16[256,512]{1,0:T(8,128)(2,1)S(1)} %collective-permute-done.5.refs_1_), channel_id=1, source_target_pairs={{0,16},{16,0},{1,17},{17,1},{2,18},{18,2},{3,19},{19,3},{4,20},{20... | collective-permute-start | bytes 786440 | tf_op jit(solution)/shard_map/ppermute | solution.py:61
  65.0 9.2 %collective-permute-start.10 = (bf16[256,512]{1,0:T(8,128)(2,1)S(1)}, bf16[256,512]{1,0:T(8,128)(2,1)S(1)}, u32[]{:S(2)}, u32[]{:S(2)}) collective-permute-start(bf16[256,512]{1,0:T(8,128)(2,1)S(1)} %collective-permute-done.6.refs_2_), channel_id=1, source_target_pairs={{0,16},{16,0},{1,17},{17,1},{2,18},{18,2},{3,19},{19,3},{4,20},{20... | collective-permute-start | bytes 786440 | tf_op jit(solution)/shard_map/ppermute | solution.py:61
  67.2 12.5 %collective-permute-start.11 = (bf16[256,512]{1,0:T(8,128)(2,1)S(1)}, bf16[256,512]{1,0:T(8,128)(2,1)S(1)}, u32[]{:S(2)}, u32[]{:S(2)}) collective-permute-start(bf16[256,512]{1,0:T(8,128)(2,1)S(1)} %collective-permute-done.7.refs_3_), channel_id=1, source_target_pairs={{0,16},{16,0},{1,17},{17,1},{2,18},{18,2},{3,19},{19,3},{4,20},{20... | collective-permute-start | bytes 786440 | tf_op jit(solution)/shard_map/ppermute | solution.py:61
  67.8 20.9 %collective-permute-start.1 = (bf16[128,2048]{1,0:T(8,128)(2,1)S(1)}, bf16[128,2048]{1,0:T(8,128)(2,1)S(1)}, u32[]{:S(2)}, u32[]{:S(2)}) collective-permute-start(bf16[128,2048]{1,0:T(8,128)(2,1)S(1)} %collective-permute-done.near), channel_id=1, source_target_pairs={{0,1},{1,0},{2,3},{3,2},{4,5},{5,4},{6,7},{7,6},{8,9},{9,8},{10,11... | collective-permute-start | bytes 1572872 | tf_op jit(solution)/shard_map/ppermute | solution.py:56
  69.3 23.9 %collective-permute-start.14 = (bf16[128,2048]{1,0:T(8,128)(2,1)S(1)}, bf16[128,2048]{1,0:T(8,128)(2,1)S(1)}, u32[]{:S(2)}, u32[]{:S(2)}) collective-permute-start(bf16[128,2048]{1,0:T(8,128)(2,1)S(1)} %collective-permute-done.13.near), channel_id=1, source_target_pairs={{0,1},{1,0},{2,3},{3,2},{4,5},{5,4},{6,7},{7,6},{8,9},{9,8},{10,11... | collective-permute-start | bytes 1572872 | tf_op jit(solution)/shard_map/ppermute | solution.py:56
  74.2 19.0 %collective-permute-start.3 = (bf16[128,2048]{1,0:T(8,128)(2,1)S(1)}, bf16[128,2048]{1,0:T(8,128)(2,1)S(1)}, u32[]{:S(2)}, u32[]{:S(2)}) collective-permute-start(bf16[128,2048]{1,0:T(8,128)(2,1)S(1)} %collective-permute-done.near), channel_id=1, source_target_pairs={{0,4},{4,0},{8,12},{12,8},{1,5},{5,1},{9,13},{13,9},{2,6},{6,2},{1... | collective-permute-start | bytes 1572872 | tf_op jit(solution)/shard_map/ppermute | solution.py:52
  79.7 8.2 %collective-permute-start.24 = (bf16[256,512]{1,0:T(8,128)(2,1)S(1)}, bf16[256,512]{1,0:T(8,128)(2,1)S(1)}, u32[]{:S(2)}, u32[]{:S(2)}) collective-permute-start(bf16[256,512]{1,0:T(8,128)(2,1)S(1)} %collective-permute-done.22.refs_4_), channel_id=1, source_target_pairs={{0,16},{16,0},{1,17},{17,1},{2,18},{18,2},{3,19},{19,3},{4,20},{20... | collective-permute-start | bytes 786440 | tf_op jit(solution)/shard_map/ppermute | solution.py:61
  88.6 28.8 %collective-permute-start.15 = (bf16[256,2048]{1,0:T(8,128)(2,1)S(1)}, bf16[256,2048]{1,0:T(8,128)(2,1)S(1)}, u32[]{:S(2)}, u32[]{:S(2)}) collective-permute-start(bf16[256,2048]{1,0:T(8,128)(2,1)S(1)} %bitcast.43), channel_id=1, source_target_pairs={{0,4},{4,0},{8,12},{12,8},{1,5},{5,1},{9,13},{13,9},{2,6},{6,2},{1... | collective-permute-start | bytes 3145736 | tf_op jit(solution)/shard_map/ppermute | solution.py:52
  88.6 7.5 %collective-permute-start.4 = (bf16[128,2048]{1,0:T(8,128)(2,1)S(1)}, bf16[128,2048]{1,0:T(8,128)(2,1)S(1)}, u32[]{:S(2)}, u32[]{:S(2)}) collective-permute-start(bf16[128,2048]{1,0:T(8,128)(2,1)S(1)} %collective-permute-done.1.far), channel_id=1, source_target_pairs={{0,4},{4,0},{8,12},{12,8},{1,5},{5,1},{9,13},{13,9},{2,6},{6,2},{1... | collective-permute-start | bytes 1572872 | tf_op jit(solution)/shard_map/ppermute | solution.py:52
  93.2 13.4 %collective-permute-start.19 = (bf16[512,512]{1,0:T(8,128)(2,1)S(1)}, bf16[512,512]{1,0:T(8,128)(2,1)S(1)}, u32[]{:S(2)}, u32[]{:S(2)}) collective-permute-start(bf16[512,512]{1,0:T(8,128)(2,1)S(1)} %get-tuple-element.77), channel_id=1, source_target_pairs={{0,4},{4,0},{8,12},{12,8},{1,5},{5,1},{9,13},{13,9},{2,6},{6,2},{1... | collective-permute-start | bytes 1572872 | tf_op jit(solution)/shard_map/ppermute | solution.py:52
  93.2 23.3 %collective-permute-start.16 = (bf16[128,2048]{1,0:T(8,128)(2,1)S(1)}, bf16[128,2048]{1,0:T(8,128)(2,1)S(1)}, u32[]{:S(2)}, u32[]{:S(2)}) collective-permute-start(bf16[128,2048]{1,0:T(8,128)(2,1)S(1)} %collective-permute-done.13.near), channel_id=1, source_target_pairs={{0,4},{4,0},{8,12},{12,8},{1,5},{5,1},{9,13},{13,9},{2,6},{6,2},{1... | collective-permute-start | bytes 1572872 | tf_op jit(solution)/shard_map/ppermute | solution.py:52
  93.7 11.8 %collective-permute-start.25 = (bf16[256,512]{1,0:T(8,128)(2,1)S(1)}, bf16[256,512]{1,0:T(8,128)(2,1)S(1)}, u32[]{:S(2)}, u32[]{:S(2)}) collective-permute-start(bf16[256,512]{1,0:T(8,128)(2,1)S(1)} %collective-permute-done.23.refs_5_), channel_id=1, source_target_pairs={{0,16},{16,0},{1,17},{17,1},{2,18},{18,2},{3,19},{19,3},{4,20},{20... | collective-permute-start | bytes 786440 | tf_op jit(solution)/shard_map/ppermute | solution.py:61
  96.1 21.7 %collective-permute-start.17 = (bf16[128,2048]{1,0:T(8,128)(2,1)S(1)}, bf16[128,2048]{1,0:T(8,128)(2,1)S(1)}, u32[]{:S(2)}, u32[]{:S(2)}) collective-permute-start(bf16[128,2048]{1,0:T(8,128)(2,1)S(1)} %collective-permute-done.14.far), channel_id=1, source_target_pairs={{0,4},{4,0},{8,12},{12,8},{1,5},{5,1},{9,13},{13,9},{2,6},{6,2},{1... | collective-permute-start | bytes 1572872 | tf_op jit(solution)/shard_map/ppermute | solution.py:52
  106.3 19.9 %collective-permute-start.20 = (bf16[512,512]{1,0:T(8,128)(2,1)S(1)}, bf16[512,512]{1,0:T(8,128)(2,1)S(1)}, u32[]{:S(2)}, u32[]{:S(2)}) collective-permute-start(bf16[512,512]{1,0:T(8,128)(2,1)S(1)} %get-tuple-element.76.refs_0_), channel_id=1, source_target_pairs={{0,16},{16,0},{1,17},{17,1},{2,18},{18,2},{3,19},{19,3},{4,20},{20... | collective-permute-start | bytes 1572872 | tf_op jit(solution)/shard_map/ppermute | solution.py:61
  106.6 25.6 %collective-permute-start.21 = (bf16[512,512]{1,0:T(8,128)(2,1)S(1)}, bf16[512,512]{1,0:T(8,128)(2,1)S(1)}, u32[]{:S(2)}, u32[]{:S(2)}) collective-permute-start(bf16[512,512]{1,0:T(8,128)(2,1)S(1)} %collective-permute-done.19.refs_1_), channel_id=1, source_target_pairs={{0,16},{16,0},{1,17},{17,1},{2,18},{18,2},{3,19},{19,3},{4,20},{20... | collective-permute-start | bytes 1572872 | tf_op jit(solution)/shard_map/ppermute | solution.py:61
  116.5 35.0 %collective-permute-start.12 = (bf16[1024,384]{1,0:T(8,128)(2,1)S(1)}, bf16[1024,384]{1,0:T(8,128)(2,1)}, u32[]{:S(2)}, u32[]{:S(2)}) collective-permute-start(bf16[1024,384]{1,0:T(8,128)(2,1)S(1)} %get-tuple-element.69.mine), channel_id=1, source_target_pairs={{0,4},{4,0},{8,12},{12,8},{1,5},{5,1},{9,13},{13,9},{2,6},{6,2},{1... | collective-permute-start | bytes 2359304 | tf_op jit(solution)/shard_map/ppermute | solution.py:52
  117.5 27.7 %collective-permute-start.28 = (bf16[256,512]{1,0:T(8,128)(2,1)}, bf16[256,512]{1,0:T(8,128)(2,1)S(1)}, u32[]{:S(2)}, u32[]{:S(2)}) collective-permute-start(bf16[256,512]{1,0:T(8,128)(2,1)} %collective-permute-done.26.refs_4_), channel_id=1, source_target_pairs={{0,16},{16,0},{1,17},{17,1},{2,18},{18,2},{3,19},{19,3},{4,20},{20... | collective-permute-start | bytes 786440 | tf_op jit(solution)/shard_map/ppermute | solution.py:61
  118.6 26.6 %collective-permute-start.29 = (bf16[256,512]{1,0:T(8,128)(2,1)}, bf16[256,512]{1,0:T(8,128)(2,1)S(1)}, u32[]{:S(2)}, u32[]{:S(2)}) collective-permute-start(bf16[256,512]{1,0:T(8,128)(2,1)} %collective-permute-done.27.refs_5_), channel_id=1, source_target_pairs={{0,16},{16,0},{1,17},{17,1},{2,18},{18,2},{3,19},{19,3},{4,20},{20... | collective-permute-start | bytes 786440 | tf_op jit(solution)/shard_map/ppermute | solution.py:61
  127.0 24.5 %collective-permute-start.18 = (bf16[1024,128]{1,0:T(8,128)(2,1)}, bf16[1024,128]{1,0:T(8,128)(2,1)}, u32[]{:S(2)}, u32[]{:S(2)}) collective-permute-start(bf16[1024,128]{1,0:T(8,128)(2,1)} %get-tuple-element.71.grad_mine), channel_id=1, source_target_pairs={{0,4},{4,0},{8,12},{12,8},{1,5},{5,1},{9,13},{13,9},{2,6},{6,2},{1... | collective-permute-start | bytes 786440 | tf_op jit(solution)/shard_map/ppermute | solution.py:52
  176.7 66.8 %collective-permute-start.38 = (bf16[512,2048]{1,0:T(8,128)(2,1)}, bf16[512,2048]{1,0:T(8,128)(2,1)}, u32[]{:S(2)}, u32[]{:S(2)}) collective-permute-start(bf16[512,2048]{1,0:T(8,128)(2,1)} %get-tuple-element.98), channel_id=1, source_target_pairs={{0,4},{4,0},{8,12},{12,8},{1,5},{5,1},{9,13},{13,9},{2,6},{6,2},{1... | collective-permute-start | bytes 6291464 | tf_op jit(solution)/shard_map/ppermute | solution.py:52
  188.1 59.4 %collective-permute-start.30 = (bf16[512,2048]{1,0:T(8,128)(2,1)}, bf16[512,2048]{1,0:T(8,128)(2,1)}, u32[]{:S(2)}, u32[]{:S(2)}) collective-permute-start(bf16[512,2048]{1,0:T(8,128)(2,1)} %get-tuple-element.87), channel_id=1, source_target_pairs={{0,4},{4,0},{8,12},{12,8},{1,5},{5,1},{9,13},{13,9},{2,6},{6,2},{1... | collective-permute-start | bytes 6291464 | tf_op jit(solution)/shard_map/ppermute | solution.py:52
  194.0 14.9 %collective-permute-start.61 = (bf16[512,512]{1,0:T(8,128)(2,1)S(1)}, bf16[512,512]{1,0:T(8,128)(2,1)S(1)}, u32[]{:S(2)}, u32[]{:S(2)}) collective-permute-start(bf16[512,512]{1,0:T(8,128)(2,1)S(1)} %bitcast.61), channel_id=1, source_target_pairs={{0,16},{16,0},{1,17},{17,1},{2,18},{18,2},{3,19},{19,3},{4,20},{20... | collective-permute-start | bytes 1572872 | tf_op jit(solution)/shard_map/ppermute | solution.py:61
  194.4 25.7 %collective-permute-start.63 = (bf16[512,512]{1,0:T(8,128)(2,1)S(1)}, bf16[512,512]{1,0:T(8,128)(2,1)S(1)}, u32[]{:S(2)}, u32[]{:S(2)}) collective-permute-start(bf16[512,512]{1,0:T(8,128)(2,1)S(1)} %bitcast.60), channel_id=1, source_target_pairs={{0,16},{16,0},{1,17},{17,1},{2,18},{18,2},{3,19},{19,3},{4,20},{20... | collective-permute-start | bytes 1572872 | tf_op jit(solution)/shard_map/ppermute | solution.py:61
  197.3 6.9 %collective-permute-start.52 = (f32[8,2048]{1,0:T(8,128)S(1)}, f32[8,2048]{1,0:T(8,128)S(1)}, u32[]{:S(2)}, u32[]{:S(2)}) collective-permute-start(f32[8,2048]{1,0:T(8,128)S(1)} %add.111), channel_id=1, source_target_pairs={{0,8},{4,12},{8,0},{12,4},{1,9},{5,13},{9,1},{13,5},{2,10},{6,14},... | collective-permute-start | bytes 196616 | tf_op jit(solution)/shard_map/ppermute | solution.py:52
  204.2 27.1 %collective-permute-start.56 = (bf16[512,512]{1,0:T(8,128)(2,1)S(1)}, bf16[512,512]{1,0:T(8,128)(2,1)S(1)}, u32[]{:S(2)}, u32[]{:S(2)}) collective-permute-start(bf16[512,512]{1,0:T(8,128)(2,1)S(1)} %bitcast.59), channel_id=1, source_target_pairs={{0,16},{16,0},{1,17},{17,1},{2,18},{18,2},{3,19},{19,3},{4,20},{20... | collective-permute-start | bytes 1572872 | tf_op jit(solution)/shard_map/ppermute | solution.py:61
  208.8 32.8 %collective-permute-start.58 = (bf16[512,512]{1,0:T(8,128)(2,1)S(1)}, bf16[512,512]{1,0:T(8,128)(2,1)S(1)}, u32[]{:S(2)}, u32[]{:S(2)}) collective-permute-start(bf16[512,512]{1,0:T(8,128)(2,1)S(1)} %bitcast.58), channel_id=1, source_target_pairs={{0,16},{16,0},{1,17},{17,1},{2,18},{18,2},{3,19},{19,3},{4,20},{20... | collective-permute-start | bytes 1572872 | tf_op jit(solution)/shard_map/ppermute | solution.py:61
  224.0 28.8 %collective-permute-start.65 = (bf16[256,512]{1,0:T(8,128)(2,1)S(1)}, bf16[256,512]{1,0:T(8,128)(2,1)S(1)}, u32[]{:S(2)}, u32[]{:S(2)}) collective-permute-start(bf16[256,512]{1,0:T(8,128)(2,1)S(1)} %get-tuple-element.119), channel_id=1, source_target_pairs={{0,12},{4,8},{8,4},{12,0},{1,13},{5,9},{9,5},{13,1},{2,14},{6,10},... | collective-permute-start | bytes 786440 | tf_op jit(solution)/shard_map/ppermute | solution.py:52
  231.3 10.9 %collective-permute-start.54 = (f32[4,2048]{1,0:T(4,128)S(1)}, f32[4,2048]{1,0:T(4,128)S(1)}, u32[]{:S(2)}, u32[]{:S(2)}) collective-permute-start(f32[4,2048]{1,0:T(4,128)S(1)} %get-tuple-element.143), channel_id=1, source_target_pairs={{0,2},{1,3},{2,0},{3,1},{4,6},{5,7},{6,4},{7,5},{8,10},{9,11},{10,... | collective-permute-start | bytes 98312 | tf_op jit(solution)/shard_map/ppermute | solution.py:56
  241.9 11.4 %collective-permute-start.60 = (bf16[256,512]{1,0:T(8,128)(2,1)S(1)}, bf16[256,512]{1,0:T(8,128)(2,1)S(1)}, u32[]{:S(2)}, u32[]{:S(2)}) collective-permute-start(bf16[256,512]{1,0:T(8,128)(2,1)S(1)} %get-tuple-element.123), channel_id=1, source_target_pairs={{0,12},{4,8},{8,4},{12,0},{1,13},{5,9},{9,5},{13,1},{2,14},{6,10},... | collective-permute-start | bytes 786440 | tf_op jit(solution)/shard_map/ppermute | solution.py:52
  242.2 14.0 %collective-permute-start.59 = (bf16[256,512]{1,0:T(8,128)(2,1)S(1)}, bf16[256,512]{1,0:T(8,128)(2,1)S(1)}, u32[]{:S(2)}, u32[]{:S(2)}) collective-permute-start(bf16[256,512]{1,0:T(8,128)(2,1)S(1)} %get-tuple-element.124), channel_id=1, source_target_pairs={{0,8},{4,12},{8,0},{12,4},{1,9},{5,13},{9,1},{13,5},{2,10},{6,14},... | collective-permute-start | bytes 786440 | tf_op jit(solution)/shard_map/ppermute | solution.py:52
  243.6 12.8 %collective-permute-start.57 = (bf16[256,512]{1,0:T(8,128)(2,1)S(1)}, bf16[256,512]{1,0:T(8,128)(2,1)S(1)}, u32[]{:S(2)}, u32[]{:S(2)}) collective-permute-start(bf16[256,512]{1,0:T(8,128)(2,1)S(1)} %get-tuple-element.134), channel_id=1, source_target_pairs={{0,4},{4,0},{8,12},{12,8},{1,5},{5,1},{9,13},{13,9},{2,6},{6,2},{1... | collective-permute-start | bytes 786440 | tf_op jit(solution)/shard_map/ppermute | solution.py:52
  247.5 41.5 %collective-permute-start.39 = (bf16[256,2048]{1,0:T(8,128)(2,1)}, bf16[256,2048]{1,0:T(8,128)(2,1)}, u32[]{:S(2)}, u32[]{:S(2)}) collective-permute-start(bf16[256,2048]{1,0:T(8,128)(2,1)} %get-tuple-element.115), channel_id=1, source_target_pairs={{0,8},{4,12},{8,0},{12,4},{1,9},{5,13},{9,1},{13,5},{2,10},{6,14},... | collective-permute-start | bytes 3145736 | tf_op jit(solution)/shard_map/ppermute | solution.py:52
  252.8 31.5 %collective-permute-start.64 = (bf16[256,512]{1,0:T(8,128)(2,1)S(1)}, bf16[256,512]{1,0:T(8,128)(2,1)S(1)}, u32[]{:S(2)}, u32[]{:S(2)}) collective-permute-start(bf16[256,512]{1,0:T(8,128)(2,1)S(1)} %get-tuple-element.120), channel_id=1, source_target_pairs={{0,8},{4,12},{8,0},{12,4},{1,9},{5,13},{9,1},{13,5},{2,10},{6,14},... | collective-permute-start | bytes 786440 | tf_op jit(solution)/shard_map/ppermute | solution.py:52
  253.3 31.5 %collective-permute-start.62 = (bf16[256,512]{1,0:T(8,128)(2,1)S(1)}, bf16[256,512]{1,0:T(8,128)(2,1)S(1)}, u32[]{:S(2)}, u32[]{:S(2)}) collective-permute-start(bf16[256,512]{1,0:T(8,128)(2,1)S(1)} %get-tuple-element.132), channel_id=1, source_target_pairs={{0,4},{4,0},{8,12},{12,8},{1,5},{5,1},{9,13},{13,9},{2,6},{6,2},{1... | collective-permute-start | bytes 786440 | tf_op jit(solution)/shard_map/ppermute | solution.py:52
  256.2 55.8 %collective-permute-start.31 = (bf16[256,2048]{1,0:T(8,128)(2,1)}, bf16[256,2048]{1,0:T(8,128)(2,1)}, u32[]{:S(2)}, u32[]{:S(2)}) collective-permute-start(bf16[256,2048]{1,0:T(8,128)(2,1)} %get-tuple-element.117), channel_id=1, source_target_pairs={{0,8},{4,12},{8,0},{12,4},{1,9},{5,13},{9,1},{13,5},{2,10},{6,14},... | collective-permute-start | bytes 3145736 | tf_op jit(solution)/shard_map/ppermute | solution.py:52
  256.4 31.9 %collective-permute-start.55 = (f32[8,2048]{1,0:T(8,128)S(1)}, f32[8,2048]{1,0:T(8,128)S(1)}, u32[]{:S(2)}, u32[]{:S(2)}) collective-permute-start(f32[8,2048]{1,0:T(8,128)S(1)} %pad_maximum_fusion), channel_id=1, source_target_pairs={{0,16},{16,0},{1,17},{17,1},{2,18},{18,2},{3,19},{19,3},{4,20},{20... | collective-permute-start | bytes 196616 | tf_op jit(solution)/shard_map/ppermute | solution.py:518
  284.3 15.1 %collective-permute-start.46 = (bf16[512,512]{1,0:T(8,128)(2,1)}, bf16[512,512]{1,0:T(8,128)(2,1)}, u32[]{:S(2)}, u32[]{:S(2)}) collective-permute-start(bf16[512,512]{1,0:T(8,128)(2,1)} %bitcast.18), channel_id=1, source_target_pairs={{0,16},{16,0},{1,17},{17,1},{2,18},{18,2},{3,19},{19,3},{4,20},{20... | collective-permute-start | bytes 1572872 | tf_op jit(solution)/shard_map/ppermute | solution.py:61
  284.8 24.9 %collective-permute-start.48 = (bf16[512,512]{1,0:T(8,128)(2,1)}, bf16[512,512]{1,0:T(8,128)(2,1)}, u32[]{:S(2)}, u32[]{:S(2)}) collective-permute-start(bf16[512,512]{1,0:T(8,128)(2,1)} %bitcast.19), channel_id=1, source_target_pairs={{0,16},{16,0},{1,17},{17,1},{2,18},{18,2},{3,19},{19,3},{4,20},{20... | collective-permute-start | bytes 1572872 | tf_op jit(solution)/shard_map/ppermute | solution.py:61
  290.6 23.0 %collective-permute-start.40 = (bf16[64,2048]{1,0:T(8,128)(2,1)S(1)}, bf16[64,2048]{1,0:T(8,128)(2,1)S(1)}, u32[]{:S(2)}, u32[]{:S(2)}) collective-permute-start(bf16[64,2048]{1,0:T(8,128)(2,1)S(1)} %get-tuple-element.100), channel_id=1, source_target_pairs={{0,1},{1,0},{2,3},{3,2},{4,5},{5,4},{6,7},{7,6},{8,9},{9,8},{10,11... | collective-permute-start | bytes 786440 | tf_op jit(solution)/shard_map/ppermute | solution.py:56
  292.2 23.0 %collective-permute-start.41 = (bf16[64,2048]{1,0:T(8,128)(2,1)S(1)}, bf16[64,2048]{1,0:T(8,128)(2,1)S(1)}, u32[]{:S(2)}, u32[]{:S(2)}) collective-permute-start(bf16[64,2048]{1,0:T(8,128)(2,1)S(1)} %get-tuple-element.101), channel_id=1, source_target_pairs={{0,2},{1,3},{2,0},{3,1},{4,6},{5,7},{6,4},{7,5},{8,10},{9,11},{10,... | collective-permute-start | bytes 786440 | tf_op jit(solution)/shard_map/ppermute | solution.py:56
  299.4 18.4 %collective-permute-start.42 = (bf16[64,2048]{1,0:T(8,128)(2,1)S(1)}, bf16[64,2048]{1,0:T(8,128)(2,1)S(1)}, u32[]{:S(2)}, u32[]{:S(2)}) collective-permute-start(bf16[64,2048]{1,0:T(8,128)(2,1)S(1)} %get-tuple-element.102), channel_id=1, source_target_pairs={{0,3},{1,2},{2,1},{3,0},{4,7},{5,6},{6,5},{7,4},{8,11},{9,10},{10,... | collective-permute-start | bytes 786440 | tf_op jit(solution)/shard_map/ppermute | solution.py:56
  311.2 38.3 %collective-permute-start.50 = (bf16[256,512]{1,0:T(8,128)(2,1)S(1)}, bf16[256,512]{1,0:T(8,128)(2,1)S(1)}, u32[]{:S(2)}, u32[]{:S(2)}) collective-permute-start(bf16[256,512]{1,0:T(8,128)(2,1)S(1)} %get-tuple-element.127), channel_id=1, source_target_pairs={{0,12},{4,8},{8,4},{12,0},{1,13},{5,9},{9,5},{13,1},{2,14},{6,10},... | collective-permute-start | bytes 786440 | tf_op jit(solution)/shard_map/ppermute | solution.py:52
  312.0 37.6 %collective-permute-start.49 = (bf16[256,512]{1,0:T(8,128)(2,1)S(1)}, bf16[256,512]{1,0:T(8,128)(2,1)S(1)}, u32[]{:S(2)}, u32[]{:S(2)}) collective-permute-start(bf16[256,512]{1,0:T(8,128)(2,1)S(1)} %get-tuple-element.128), channel_id=1, source_target_pairs={{0,8},{4,12},{8,0},{12,4},{1,9},{5,13},{9,1},{13,5},{2,10},{6,14},... | collective-permute-start | bytes 786440 | tf_op jit(solution)/shard_map/ppermute | solution.py:52
  313.6 14.6 %collective-permute-start.32 = (bf16[64,2048]{1,0:T(8,128)(2,1)S(1)}, bf16[64,2048]{1,0:T(8,128)(2,1)S(1)}, u32[]{:S(2)}, u32[]{:S(2)}) collective-permute-start(bf16[64,2048]{1,0:T(8,128)(2,1)S(1)} %get-tuple-element.89), channel_id=1, source_target_pairs={{0,1},{1,0},{2,3},{3,2},{4,5},{5,4},{6,7},{7,6},{8,9},{9,8},{10,11... | collective-permute-start | bytes 786440 | tf_op jit(solution)/shard_map/ppermute | solution.py:56
  315.2 21.4 %collective-permute-start.33 = (bf16[64,2048]{1,0:T(8,128)(2,1)S(1)}, bf16[64,2048]{1,0:T(8,128)(2,1)S(1)}, u32[]{:S(2)}, u32[]{:S(2)}) collective-permute-start(bf16[64,2048]{1,0:T(8,128)(2,1)S(1)} %get-tuple-element.90), channel_id=1, source_target_pairs={{0,2},{1,3},{2,0},{3,1},{4,6},{5,7},{6,4},{7,5},{8,10},{9,11},{10,... | collective-permute-start | bytes 786440 | tf_op jit(solution)/shard_map/ppermute | solution.py:56
  317.8 21.3 %collective-permute-start.34 = (bf16[64,2048]{1,0:T(8,128)(2,1)S(1)}, bf16[64,2048]{1,0:T(8,128)(2,1)S(1)}, u32[]{:S(2)}, u32[]{:S(2)}) collective-permute-start(bf16[64,2048]{1,0:T(8,128)(2,1)S(1)} %get-tuple-element.91), channel_id=1, source_target_pairs={{0,3},{1,2},{2,1},{3,0},{4,7},{5,6},{6,5},{7,4},{8,11},{9,10},{10,... | collective-permute-start | bytes 786440 | tf_op jit(solution)/shard_map/ppermute | solution.py:56
  328.2 22.9 %collective-permute-start.47 = (bf16[256,512]{1,0:T(8,128)(2,1)S(1)}, bf16[256,512]{1,0:T(8,128)(2,1)S(1)}, u32[]{:S(2)}, u32[]{:S(2)}) collective-permute-start(bf16[256,512]{1,0:T(8,128)(2,1)S(1)} %get-tuple-element.136), channel_id=1, source_target_pairs={{0,4},{4,0},{8,12},{12,8},{1,5},{5,1},{9,13},{13,9},{2,6},{6,2},{1... | collective-permute-start | bytes 786440 | tf_op jit(solution)/shard_map/ppermute | solution.py:52
  336.6 16.5 %collective-permute-start.45 = (bf16[64,2048]{1,0:T(8,128)(2,1)S(1)}, bf16[64,2048]{1,0:T(8,128)(2,1)S(1)}, u32[]{:S(2)}, u32[]{:S(2)}) collective-permute-start(bf16[64,2048]{1,0:T(8,128)(2,1)S(1)} %add_convert_fusion.16.refs_0_), channel_id=1, source_target_pairs={{0,3},{1,2},{2,1},{3,0},{4,7},{5,6},{6,5},{7,4},{8,11},{9,10},{10,... | collective-permute-start | bytes 786440 | tf_op jit(solution)/shard_map/ppermute | solution.py:56
  339.1 37.0 %collective-permute-start.44 = (bf16[64,2048]{1,0:T(8,128)(2,1)S(1)}, bf16[64,2048]{1,0:T(8,128)(2,1)}, u32[]{:S(2)}, u32[]{:S(2)}) collective-permute-start(bf16[64,2048]{1,0:T(8,128)(2,1)S(1)} %add_convert_fusion.16.refs_0_), channel_id=1, source_target_pairs={{0,2},{1,3},{2,0},{3,1},{4,6},{5,7},{6,4},{7,5},{8,10},{9,11},{10,... | collective-permute-start | bytes 786440 | tf_op jit(solution)/shard_map/ppermute | solution.py:56
  349.6 26.5 %collective-permute-start.43 = (bf16[64,2048]{1,0:T(8,128)(2,1)S(1)}, bf16[64,2048]{1,0:T(8,128)(2,1)}, u32[]{:S(2)}, u32[]{:S(2)}) collective-permute-start(bf16[64,2048]{1,0:T(8,128)(2,1)S(1)} %add_convert_fusion.16.refs_0_), channel_id=1, source_target_pairs={{0,1},{1,0},{2,3},{3,2},{4,5},{5,4},{6,7},{7,6},{8,9},{9,8},{10,11... | collective-permute-start | bytes 786440 | tf_op jit(solution)/shard_map/ppermute | solution.py:56
  349.7 31.2 %collective-permute-start.37 = (bf16[64,2048]{1,0:T(8,128)(2,1)S(1)}, bf16[64,2048]{1,0:T(8,128)(2,1)S(1)}, u32[]{:S(2)}, u32[]{:S(2)}) collective-permute-start(bf16[64,2048]{1,0:T(8,128)(2,1)S(1)} %add_convert_fusion.17.refs_0_), channel_id=1, source_target_pairs={{0,3},{1,2},{2,1},{3,0},{4,7},{5,6},{6,5},{7,4},{8,11},{9,10},{10,... | collective-permute-start | bytes 786440 | tf_op jit(solution)/shard_map/ppermute | solution.py:56
  351.1 36.0 %collective-permute-start.36 = (bf16[64,2048]{1,0:T(8,128)(2,1)S(1)}, bf16[64,2048]{1,0:T(8,128)(2,1)}, u32[]{:S(2)}, u32[]{:S(2)}) collective-permute-start(bf16[64,2048]{1,0:T(8,128)(2,1)S(1)} %add_convert_fusion.17.refs_0_), channel_id=1, source_target_pairs={{0,2},{1,3},{2,0},{3,1},{4,6},{5,7},{6,4},{7,5},{8,10},{9,11},{10,... | collective-permute-start | bytes 786440 | tf_op jit(solution)/shard_map/ppermute | solution.py:56
  353.1 34.0 %collective-permute-start.35 = (bf16[64,2048]{1,0:T(8,128)(2,1)S(1)}, bf16[64,2048]{1,0:T(8,128)(2,1)}, u32[]{:S(2)}, u32[]{:S(2)}) collective-permute-start(bf16[64,2048]{1,0:T(8,128)(2,1)S(1)} %add_convert_fusion.17.refs_0_), channel_id=1, source_target_pairs={{0,1},{1,0},{2,3},{3,2},{4,5},{5,4},{6,7},{7,6},{8,9},{9,8},{10,11... | collective-permute-start | bytes 786440 | tf_op jit(solution)/shard_map/ppermute | solution.py:56
  (74 other events, 926.3 us)
